TPU v7x, 32 devices: a whole 2x2x4 slice. The times are simulated.
32 devices in a mesh: groups: 2 (over x), layer: 16 (over z, y, core).
Axes of the slice: x: 2, y: 2, z: 4, core: 2. Of those that a mesh axis runs over, the one named last changes fastest.
Arguments:
- token_ids: int32 [16, 64], P('groups'), parts along dimension 0, may hold values from 0 to 2047
- hidden_pool: bfloat16 [4096, 16384], P('groups', 'layer'), parts along dimension 0, may hold values from -6 to 6
- basis: bfloat16 [16384, 8192], P('layer', 'groups'), parts along dimension 1, may hold values from -0.046875 to 0.046875
- coeffs: bfloat16 [8, 8192, 16384], P(None, 'groups', 'layer'), parts along dimension 1, may hold values from -0.09375 to 0.09375
- targets: bfloat16 [16, 64, 16384], P('groups', None, 'layer'), parts along dimension 0, may hold values from -6 to 6
Outputs:
- residual: float32 [16, 64, 16384], P('groups', None, 'layer'), parts along dimension 0
- basis_grad: float32 [16384, 8192], P('layer', 'groups'), parts along dimension 1
There are 2 independent parts, one for each index of `groups`. A program takes and returns all parts, laid end to end along the dimension named above; each array names one. Nothing has to cross between parts.
All inputs are finite; a program needn't handle non-finite values.
Results may differ from a plain program's by a relative error of at most 0.0041.
Values may be sent and summed in bfloat16 or wider, within the bound.
No kernel may reach another device: no remote copies, remote signals or barrier semaphores. Data moves between devices by JAX's collectives and lax.ppermute only.
A program may use at most 256 MiB of HBM per device.

v0:
```python
import jax
import jax.numpy as jnp
from jax import lax
from jax.sharding import PartitionSpec as P


def on_device(token_ids, hidden_pool, basis, coeffs, targets):
    layer_count, tok_count = token_ids.shape
    row_count = layer_count * tok_count
    rank_total = basis.shape[1]
    x_local = jnp.take(hidden_pool, token_ids.reshape(-1), axis=0)
    proj_share = lax.psum_scatter(
        lax.dot_general(
            basis, x_local, (((0,), (1,)), ((), ())), preferred_element_type=jnp.float32
        ),
        "layer",
        scatter_dimension=0,
        tiled=True,
    ).astype(jnp.bfloat16)
    piece = lax.all_gather(proj_share, "layer", axis=0, tiled=True)
    piece_rows = piece.shape[0]
    coeff_part = coeffs
    shaped = piece.reshape(piece_rows, layer_count, tok_count)
    predicted = jnp.einsum("kls,lko->lso", shaped, coeff_part, preferred_element_type=jnp.float32)
    residual = targets.astype(jnp.float32) - predicted
    res_low = residual.astype(jnp.bfloat16)
    coeff_part = coeffs
    summed = jnp.einsum("lko,lso->kls", coeff_part, res_low, preferred_element_type=jnp.float32)
    back_whole = lax.psum(summed.reshape(rank_total, row_count), "layer").astype(jnp.bfloat16)
    product = lax.dot_general(
        x_local, back_whole, (((0,), (1,)), ((), ())), preferred_element_type=jnp.float32
    )
    grad = product * (-1.0 / tok_count)
    return (residual, grad)


def solution(mesh):
    placed = (
        P("groups", None),
        P("groups", "layer"),
        P("layer", "groups"),
        P(None, "groups", "layer"),
        P("groups", None, "layer"),
    )
    return jax.shard_map(
        on_device,
        mesh=mesh,
        in_specs=placed,
        out_specs=(P("groups", None, "layer"), P("layer", "groups")),
        check_vma=False,
    )
```

profile of v0, /device:TPU:0, one launch (start us, length us, event | category | flops | bytes accessed | tf_op | source)
XLA Modules:
  0.0 443.9 jit_solution(14973202244128177244)
XLA Ops:
  7.2 0.0 reduce-scatter.2.cloned.1.call-start
  7.2 0.8 reshape.50
  8.0 0.8 reshape.49
  8.8 5.5 %gather_fusion = bf16[512,1024]{1,0:T(8,128)(2,1)S(1)} fusion(bf16[2048,1024]{1,0:T(8,128)(2,1)} %param.6, s32[1024]{0:T(1024)S(1)} %pad_clamp_fusion), kind=kCustom, calls=%fused_computation | custom fusion | bytes 2099200 | tf_op jit(solution)/shard_map/jit(_take)/gather | solution.py:11
  14.2 0.0 copy-start.2
  14.2 1.0 copy-done.2
  15.2 10.3 %convolution_bitcast_fusion = f32[4096,512]{0,1:T(8,128)} fusion(bf16[1024,4096]{1,0:T(8,128)(2,1)} %param.7, bf16[512,1024]{1,0:T(8,128)(2,1)S(1)} %gather_fusion, pred[512]{0:T(512)(128)(4,1)S(1)} %compare_and_fusion), kind=kOutput, calls=%fused_computation.2 | convolution fusion | flops 4295491584 | bytes 17826304 | tf_op jit(solution)/shard_map/dot_general | solution.py:13
  25.5 0.0 copy-start.1
  25.5 0.0 reduce-scatter.2.cloned.1.call-update
  25.5 0.0 all-gather.2.cloned.1.call-start
  25.6 107.7 %reduce-scatter.2.cloned.1.call-done = f32[256,512]{0,1:T(8,128)} async-done(((f32[4096,512]{0,1:T(8,128)}), f32[256,512]{0,1:T(8,128)}) %reduce-scatter.2.cloned.1.call-update) | async-done | bytes 524304 | tf_op jit(solution)/shard_map/reduce_scatter | solution.py:12
  133.2 1.8 convert_element_type.13
  135.0 0.0 all-gather.2.cloned.1.call-update
  135.0 53.9 %all-gather.2.cloned.1.call-done = bf16[4096,512]{0,1:T(8,128)(2,1)} async-done(((bf16[256,512]{0,1:T(8,128)(2,1)}), bf16[4096,512]{0,1:T(8,128)(2,1)}) %all-gather.2.cloned.1.call-update) | async-done | bytes 4194320 | tf_op jit(solution)/shard_map/all_gather | solution.py:20
  188.9 0.0 copy-done.1
  189.0 24.5 %convert_subtract_fusion = f32[8,64,1024]{2,1,0:T(8,128)S(1)} fusion(bf16[8,64,1024]{2,1,0:T(8,128)(2,1)S(1)} %copy-done.1, bf16[4096,8,64]{0,2,1:T(8,128)(2,1)} %bitcast.12, bf16[8,4096,1024]{2,1,0:T(8,128)(2,1)} %param.8), kind=kOutput, calls=%fused_computation.4 | convolution fusion | flops 4296015872 | bytes 74448896 | tf_op jit(solution)/shard_map/kls,lko->lso/dot_general | solution.py:24
  213.5 0.0 copy-start
  213.5 31.5 %fusion.1 = f32[8,64,4096]{2,1,0:T(8,128)} fusion(bf16[8,4096,1024]{2,1,0:T(8,128)(2,1)} %param.8, f32[8,64,1024]{2,1,0:T(8,128)S(1)} %convert_subtract_fusion), kind=kOutput, calls=%fused_computation.5 | convolution fusion | flops 4295491584 | bytes 77594624 | tf_op jit(solution)/shard_map/lko,lso->kls/dot_general | solution.py:28
  245.0 0.0 copy-done
  245.0 0.0 copy-start.3
  245.0 181.2 %all-reduce.1 = bf16[4096,512]{0,1:T(8,128)(2,1)} all-reduce(f32[4096,512]{0,1:T(8,128)} %bitcast.13), channel_id=1, replica_groups=mesh['groups'=2,'layer'=16] {'layer'}, use_global_device_ids=true, to_apply=%region_1.2 | all-reduce | flops 2097152 | bytes 12582912 | tf_op jit(solution)/shard_map/psum | solution.py:29
  426.2 0.0 copy-done.3
  426.2 10.8 %convolution_multiply_fusion = f32[1024,4096]{1,0:T(8,128)} fusion(bf16[4096,512]{0,1:T(8,128)(2,1)} %all-reduce.1, bf16[512,1024]{1,0:T(8,128)(2,1)S(1)} %copy-done.3, pred[512]{0:T(512)(128)(4,1)S(1)} %compare_and_fusion), kind=kOutput, calls=%fused_computation.1 | convolution fusion | flops 4299685888 | bytes 22020608 | tf_op jit(solution)/shard_map/dot_general | solution.py:30
  (3 shorter events, 0.0 us)
Async XLA Ops:
  7.2 126.1 %reduce-scatter.2.cloned.1.call-start = ((), (), s32[]{:S(2)}) async-start(), calls=%async_computation.1 | async-start | bytes 8912896 | tf_op jit(solution)/shard_map/reduce_scatter | solution.py:12
  14.2 1.0 copy-start.2
  25.5 163.5 %copy-start.1 = (bf16[8,64,1024]{2,1,0:T(8,128)(2,1)S(1)}, bf16[8,64,1024]{2,1,0:T(8,128)(2,1)}, u32[]{:S(2)}) copy-start(bf16[8,64,1024]{2,1,0:T(8,128)(2,1)} %param.9) | copy-start | bytes 3145732
  25.5 163.4 %all-gather.2.cloned.1.call-start = ((), (), s32[]{:S(2)}) async-start(), calls=%async_computation.2 | async-start | bytes 4456448 | tf_op jit(solution)/shard_map/all_gather | solution.py:20
  213.5 31.5 %copy-start = (f32[8,64,1024]{2,1,0:T(8,128)}, f32[8,64,1024]{2,1,0:T(8,128)S(1)}, u32[]{:S(2)}) copy-start(f32[8,64,1024]{2,1,0:T(8,128)S(1)} %convert_subtract_fusion) | copy-start | bytes 6291460
  245.0 181.2 %copy-start.3 = (bf16[512,1024]{1,0:T(8,128)(2,1)S(1)}, bf16[512,1024]{1,0:T(8,128)(2,1)}, u32[]{:S(2)}) copy-start(bf16[512,1024]{1,0:T(8,128)(2,1)} %copy-done.2) | copy-start | bytes 3145732
Sparse Core Ops, SparseCore 0:
  25.6 107.5 reduce-scatter.1
  135.9 52.9 all-gather.1
where the time goes:
time: 446 us; the launch traced here: 444 us
  blocking collectives  181 us (41%)
  waiting for transfers between devices  162 us (36%)
  matrix products  77.1 us (17%)
  between operations  14.1 us (3%)
  local copies, waits for them, and re-layouts  7.97 us (2%)
    psum x1, blocking collectives, on_device(): lax.psum(summed.reshape(rank_total, row_count), 'layer')  181 us
    reduce_scatter x1, waiting for transfers between devices, on_device(): lax.psum_scatter(lax.dot_general(basis, x_local, (((0,), (1,)), ((), ()))...  108 us
    all_gather x1, waiting for transfers between devices, on_device(): piece = lax.all_gather(proj_share, 'layer', axis=0, tiled=True)  53.9 us
    dot_general x1, matrix products, on_device(): jnp.einsum('lko,lso->kls', coeff_part, res_low, preferred_element_type=jn...  31.5 us
    dot_general x1, matrix products, on_device(): jnp.einsum('kls,lko->lso', shaped, coeff_part, preferred_element_type=jnp...  24.5 us
    dot_general x1, matrix products, on_device(): lax.dot_general(x_local, back_whole, (((0,), (1,)), ((), ())), preferred_...  10.8 us
    dot_general x1, matrix products, on_device(): lax.dot_general(basis, x_local, (((0,), (1,)), ((), ())), preferred_eleme...  10.3 us
  transfers between devices with their start and end apart: 2, of which 2 were waited for; matrix products, arithmetic and copies ran while one was open for 0% of the time, Pallas kernels for 0%

commit v1 on v0

v1 whole, which is shorter than its diff:
```python
import functools
import math

import jax
import jax.numpy as jnp
from jax import lax
from jax.experimental import pallas as pl
from jax.experimental.pallas import tpu as pltpu
from jax.sharding import PartitionSpec as P

X_MAX = 6.0
BASIS_MAX = 0.046875
F32 = jnp.float32
BF16 = jnp.bfloat16
F16 = jnp.float16
IN_VMEM = pl.BlockSpec(memory_space=pltpu.MemorySpace.VMEM)
IN_SMEM = pl.BlockSpec(memory_space=pltpu.MemorySpace.SMEM)
IN_HBM = pl.BlockSpec(memory_space=pltpu.MemorySpace.HBM)
MIB = 2**20


def params(mib):
    return pltpu.CompilerParams(vmem_limit_bytes=mib * MIB)


def cost(flops, moved):
    return pl.CostEstimate(flops=flops, bytes_accessed=moved, transcendentals=0)


def block(ref, i, size):
    return pl.ds(pl.multiple_of(ref[i] * size, size), size)


def join(value, mark):
    return pl.pallas_call(
        lambda value_ref, mark_ref, out_ref: None,
        out_shape=jax.ShapeDtypeStruct(value.shape, value.dtype),
        in_specs=[IN_VMEM, IN_VMEM],
        out_specs=IN_VMEM,
        input_output_aliases={0: 0},
        compiler_params=params(2),
        name="join",
    )(value, mark)


def start_body(cols, kb, idx_ref, hot_ref, pool_ref, basis_ref, x_ref, tiles_ref, sems):
    n = tiles_ref.shape[0]

    def tile(i):
        return pltpu.make_async_copy(basis_ref.at[:, block(idx_ref, i, kb)], tiles_ref.at[i], sems.at[i])

    for i in range(n):
        tile(i).start()

    @pl.loop(0, x_ref.shape[1] // cols)
    def _(i):
        window = pl.ds(pl.multiple_of(i * cols, cols), cols)
        x_ref[:, window] = jnp.dot(
            hot_ref[...], pool_ref[:, window], preferred_element_type=F32
        ).astype(BF16)

    @pl.loop(0, n)
    def _(i):
        tile(i).wait()


def start(idx, ids, pool, basis, kb):
    rows = ids.shape[0]
    pool_rows, depth = pool.shape
    n = idx.shape[0]
    hot = (ids == lax.broadcasted_iota(jnp.int32, (rows, pool_rows), 1)).astype(BF16)
    return pl.pallas_call(
        functools.partial(start_body, 256, kb),
        out_shape=(
            jax.ShapeDtypeStruct((rows, depth), BF16),
            jax.ShapeDtypeStruct((n, depth, kb), BF16),
        ),
        in_specs=[IN_SMEM, IN_VMEM, IN_VMEM, IN_HBM],
        out_specs=(IN_VMEM, IN_VMEM),
        scratch_shapes=[pltpu.SemaphoreType.DMA((n,))],
        compiler_params=params(36),
        cost_estimate=cost(2 * rows * pool_rows * depth, pool_rows * depth * 2),
        name="start",
    )(idx, hot, pool, basis)


def project_body(first, sizes, x_ref, tiles_ref, mark_ref, *outs):
    base = first
    for out, size in zip(outs, sizes):

        @pl.loop(0, size)
        def _(j, base=base, out=out):
            out[j] = jnp.dot(x_ref[...], tiles_ref[base + j], preferred_element_type=F32)

        base += size


def project(first, sizes, x, tiles, mark):
    rows, depth = x.shape
    kb = tiles.shape[2]
    n = sum(sizes)
    return pl.pallas_call(
        functools.partial(project_body, first, sizes),
        out_shape=tuple(jax.ShapeDtypeStruct((size, rows, kb), F32) for size in sizes),
        in_specs=[IN_VMEM, IN_VMEM, IN_VMEM],
        out_specs=(IN_VMEM,) * len(sizes),
        compiler_params=params(8),
        cost_estimate=cost(2 * n * rows * depth * kb, n * depth * kb * 2),
        name="project",
    )(x, tiles, mark)


def finish(keep, other, to_right, to_left):
    _, kb, rows = keep.shape

    def body(keep_ref, other_ref, right_ref, left_ref, out_ref):
        total = keep_ref[0] + other_ref[0] + right_ref[...].astype(F32) + left_ref[...].astype(F32)
        out_ref[...] = total.T.astype(BF16)

    return pl.pallas_call(
        body,
        out_shape=jax.ShapeDtypeStruct((rows, kb), BF16),
        in_specs=[IN_VMEM] * 4,
        out_specs=IN_VMEM,
        compiler_params=params(8),
        name="finish",
    )(keep, other, to_right, to_left)


def coeff_copy(idx_ref, coeff_ref, buf, sems, kb, l, i):
    return pltpu.make_async_copy(
        coeff_ref.at[l, block(idx_ref, i, kb), :], buf.at[l, pl.ds(i * kb, kb), :], sems.at[l, i]
    )


def start_coeffs(idx_ref, coeff_ref, buf, sems, n, kb):
    @pl.loop(0, buf.shape[0])
    def _(l):
        for i in range(n):
            coeff_copy(idx_ref, coeff_ref, buf, sems, kb, l, i).start()


def wait_coeffs(idx_ref, coeff_ref, buf, sems, n, kb, l):
    for i in range(n):
        coeff_copy(idx_ref, coeff_ref, buf, sems, kb, l, i).wait()


def rows_of(l, size):
    return pl.ds(pl.multiple_of(l * size, size), size)


def wide(pieces, span):
    return jnp.concatenate([piece[span, :] for piece in pieces], axis=1)


def predict_body(n, first, idx_ref, coeff_ref, *refs):
    pieces, rest = refs[:n], refs[n:]
    if first:
        out_ref, mark_ref, buf, sems = rest
    else:
        acc_ref, out_ref, mark_ref, buf, sems = rest
    layer_count = buf.shape[0]
    mark_ref[...] = jnp.zeros_like(mark_ref)
    rows, kb = pieces[0].shape
    toks = rows // layer_count
    start_coeffs(idx_ref, coeff_ref, buf, sems, n, kb)

    @pl.loop(0, layer_count)
    def _(l):
        span = rows_of(l, toks)
        wait_coeffs(idx_ref, coeff_ref, buf, sems, n, kb, l)
        part = jnp.dot(wide(pieces, span), buf[l], preferred_element_type=F32)
        out_ref[span, :] = part if first else acc_ref[span, :] + part


def coeff_scratch(coeffs, n, kb):
    layer_count, _, width = coeffs.shape
    return [pltpu.VMEM((layer_count, n * kb, width), BF16), pltpu.SemaphoreType.DMA((layer_count, n))]


def predict(idx, coeffs, pieces, acc):
    n = len(pieces)
    rows, kb = pieces[0].shape
    layer_count, _, width = coeffs.shape
    first = acc is None
    return pl.pallas_call(
        functools.partial(predict_body, n, first),
        out_shape=(jax.ShapeDtypeStruct((rows, width), F32), jax.ShapeDtypeStruct((8, 128), F32)),
        in_specs=[IN_SMEM, IN_HBM] + [IN_VMEM] * (n + (not first)),
        out_specs=(IN_VMEM, IN_VMEM),
        input_output_aliases={} if first else {n + 2: 0},
        scratch_shapes=coeff_scratch(coeffs, n, kb),
        compiler_params=params(4 * n + 3),
        cost_estimate=cost(8 * n * rows * kb * width, layer_count * n * kb * width * 2),
        name="predict",
    )(idx, coeffs, *pieces, *([] if first else [acc]))


def back_blocks(low, buf, l, keep_ref, send_ref, toks):
    m, kb, _ = keep_ref.shape
    parts = [
        lax.dot_general(
            buf[l + j],
            low[j * toks : (j + 1) * toks, :],
            (((1,), (1,)), ((), ())),
            preferred_element_type=F32,
        )
        for j in range(2)
    ]
    both = jnp.concatenate(parts, axis=1)
    lanes = pl.ds(pl.multiple_of(l * toks, 2 * toks), 2 * toks)
    for i in range(m):
        keep_ref[i, :, lanes] = both[i * kb : (i + 1) * kb, :]
        send_ref[i, :, lanes] = both[(m + i) * kb : (m + i + 1) * kb, :]


def residual_body(n, idx_ref, coeff_ref, *refs):
    pieces, (target_ref, acc_ref, res_ref, low_ref, keep_ref, send_ref, buf, sems) = refs[:n], refs[n:]
    layer_count = buf.shape[0]
    rows, kb = pieces[0].shape
    toks = rows // layer_count
    start_coeffs(idx_ref, coeff_ref, buf, sems, n, kb)

    @pl.loop(0, layer_count, step=2)
    def _(l):
        for j in range(2):
            span = rows_of(l + j, toks)
            wait_coeffs(idx_ref, coeff_ref, buf, sems, n, kb, l + j)
            part = jnp.dot(wide(pieces, span), buf[l + j], preferred_element_type=F32)
            res = target_ref[l + j].astype(F32) - (acc_ref[span, :] + part)
            res_ref[l + j] = res
            low_ref[span, :] = res.astype(BF16)
        pair = pl.ds(pl.multiple_of(l * toks, 2 * toks), 2 * toks)
        back_blocks(low_ref[pair, :], buf, l, keep_ref, send_ref, toks)


def residuals(idx, coeffs, pieces, targets, acc):
    n = len(pieces)
    rows, kb = pieces[0].shape
    layer_count, _, width = coeffs.shape
    half = jax.ShapeDtypeStruct((n // 2, kb, rows), F32)
    return pl.pallas_call(
        functools.partial(residual_body, n),
        out_shape=(
            jax.ShapeDtypeStruct(targets.shape, F32),
            jax.ShapeDtypeStruct((rows, width), BF16),
            half,
            half,
        ),
        in_specs=[IN_SMEM, IN_HBM] + [IN_VMEM] * (n + 2),
        out_specs=(IN_VMEM,) * 4,
        scratch_shapes=coeff_scratch(coeffs, n, kb),
        compiler_params=params(4 * n + 3),
        cost_estimate=cost(16 * n * rows * kb * width, layer_count * n * kb * width * 2),
        name="residuals",
    )(idx, coeffs, *pieces, targets, acc)


def backward_body(n, idx_ref, coeff_ref, low_ref, mark_ref, keep_ref, send_ref, buf, sems):
    layer_count = buf.shape[0]
    kb = keep_ref.shape[1]
    toks = low_ref.shape[0] // layer_count
    start_coeffs(idx_ref, coeff_ref, buf, sems, n, kb)

    @pl.loop(0, layer_count, step=2)
    def _(l):
        for j in range(2):
            wait_coeffs(idx_ref, coeff_ref, buf, sems, n, kb, l + j)
        pair = pl.ds(pl.multiple_of(l * toks, 2 * toks), 2 * toks)
        back_blocks(low_ref[pair, :], buf, l, keep_ref, send_ref, toks)


def backward(idx, coeffs, low, mark, kb):
    n = idx.shape[0]
    rows = low.shape[0]
    layer_count, _, width = coeffs.shape
    half = jax.ShapeDtypeStruct((n // 2, kb, rows), F32)
    return pl.pallas_call(
        functools.partial(backward_body, n),
        out_shape=(half, half),
        in_specs=[IN_SMEM, IN_HBM, IN_VMEM, IN_VMEM],
        out_specs=(IN_VMEM,) * 2,
        scratch_shapes=coeff_scratch(coeffs, n, kb),
        compiler_params=params(4 * n + 3),
        cost_estimate=cost(8 * n * rows * kb * width, layer_count * n * kb * width * 2),
        name="backward",
    )(idx, coeffs, low, mark)


def gradient_body(n, scale, first, idx_ref, xt_ref, *refs):
    pieces, (out_ref, mark_ref, buf, sems) = refs[:n], refs[n + (not first) :]
    mark_ref[...] = jnp.zeros_like(mark_ref)
    kb = buf.shape[2]
    depth = buf.shape[1]
    copies = []
    for i in range(n):

        @pl.loop(0, 2)
        def _(r, i=i):
            span = rows_of(r, depth // 2)
            buf[i, span, :] = jnp.dot(xt_ref[span, :], pieces[i][...], preferred_element_type=F32) * scale

        copies.append(
            pltpu.make_async_copy(buf.at[i], out_ref.at[:, block(idx_ref, i, kb)], sems.at[i])
        )
        copies[-1].start()
    for copy in copies:
        copy.wait()


def gradient(idx, xt, pieces, grad, width, scale):
    n = len(pieces)
    kb = pieces[0].shape[1]
    depth, rows = xt.shape
    first = grad is None
    return pl.pallas_call(
        functools.partial(gradient_body, n, scale, first),
        out_shape=(jax.ShapeDtypeStruct((depth, width), F32), jax.ShapeDtypeStruct((8, 128), F32)),
        in_specs=[IN_SMEM] + [IN_VMEM] * (n + 1) + [IN_HBM] * (not first),
        out_specs=(IN_HBM, IN_VMEM),
        input_output_aliases={} if first else {n + 2: 0},
        scratch_shapes=[pltpu.VMEM((n, depth, kb), F32), pltpu.SemaphoreType.DMA((n,))],
        compiler_params=params(16),
        cost_estimate=cost(2 * n * depth * rows * kb, n * depth * kb * 4),
        name="gradient",
    )(idx, xt, *pieces, *([] if first else [grad]))


def plain(token_ids, hidden_pool, basis, coeffs, targets):
    layer_count, tok_count = token_ids.shape
    x_local = jnp.take(hidden_pool, token_ids.reshape(-1), axis=0)
    share = lax.psum_scatter(
        lax.dot_general(basis, x_local, (((0,), (1,)), ((), ())), preferred_element_type=F32),
        "layer",
        scatter_dimension=0,
        tiled=True,
    ).astype(BF16)
    piece = lax.all_gather(share, "layer", axis=0, tiled=True)
    shaped = piece.reshape(piece.shape[0], layer_count, tok_count)
    predicted = jnp.einsum("kls,lko->lso", shaped, coeffs, preferred_element_type=F32)
    residual = targets.astype(F32) - predicted
    summed = jnp.einsum("lko,lso->kls", coeffs, residual.astype(BF16), preferred_element_type=F32)
    summed = summed.reshape(basis.shape[1], -1)
    back = lax.psum_scatter(summed, "layer", scatter_dimension=0, tiled=True).astype(BF16)
    back = lax.all_gather(back, "layer", axis=0, tiled=True)
    product = lax.dot_general(x_local, back, (((0,), (1,)), ((), ())), preferred_element_type=F32)
    return residual, product * (-1.0 / tok_count)


def staged(zn, token_ids, hidden_pool, basis, coeffs, targets):
    chips = 2 * zn
    tok_count = token_ids.shape[1]
    rank = basis.shape[1]
    kb = rank // (2 * chips)
    me = lax.axis_index("layer")
    core, y, z = me % 2, (me // 2) % 2, me // 4
    place = jnp.where(y == 0, z, chips - 1 - z)
    order = [2 * z for z in range(zn)] + [2 * z + 1 for z in reversed(range(zn))]

    def turn(step):
        return [
            (2 * order[i] + c, 2 * order[(i + step) % chips] + c) for i in range(chips) for c in range(2)
        ]

    right, left = turn(1), turn(-1)
    across = [(i, i ^ 1) for i in range(2 * chips)]

    def send(a, pairs):
        return lax.ppermute(a, "layer", pairs)

    def index(half, i):
        return (core ^ half) * chips + (place + i) % chips

    far = chips // 2
    rounds = [[far]] + [[i, chips - i] for i in range(far - 1, 0, -1)] + [[0]]

    def both(items):
        return jnp.stack([index(h, i) for h in range(2) for i in items]).astype(jnp.int32)

    def scatter_sum(parts, wire, scale, last):
        keeps, others = [], []

        def mine(r, j):
            return (keeps[r][j] + others[r][j]) * scale

        def blocks(r, mark):
            keep, out = parts[r](mark)
            keeps.append(keep)
            return out

        def swap(out, mark):
            others.append(send(out if mark is None else join(out, mark), across))

        def corner(message):
            return message[:8, :128].astype(F32)

        swap(blocks(0, None), None)
        out = blocks(1, None)
        first = mine(0, 0).astype(wire)
        cut = first.shape[0] // 2
        to_right, to_left = send(first[:cut], right), send(first[cut:], left)
        for r in range(1, far):
            mark = corner(first)
            swap(out, mark)
            out = blocks(r + 1, mark)
            a, b = mine(r, 0), mine(r, 1)
            if r == 1:
                a = jnp.concatenate([a[:cut] + to_right.astype(F32), a[cut:]])
                b = jnp.concatenate([b[:cut], b[cut:] + to_left.astype(F32)])
            else:
                a, b = a + to_right.astype(F32), b + to_left.astype(F32)
            first, second = a.astype(wire), b.astype(wire)
            to_right, to_left = send(first, right), send(second, left)
        swap(out, corner(first))
        return last(keeps[far], others[far], to_right, to_left)

    def gather(own, use, lag):
        a, b = send(own, right), send(own, left)
        came = [([(0, 0)], [own])]
        waiting = [([(1, 0)], [send(own, across)])]
        cut = own.shape[0] // 2
        for i in range(1, far):
            if not lag:
                came, waiting = came + waiting, []
            mark = use(sum([c[0] for c in came], []), sum([c[1] for c in came], []))
            came, waiting = waiting, []
            a = join(a, mark)
            places, got = [chips - i, i], [a, b]
            if i < far - 1:
                a, b = send(a, right), send(b, left)
            else:
                a, b = send(a[:cut], right), send(b[cut:], left)
            came.append(([(0, p) for p in places], got))
            waiting.append(([(1, p) for p in places], [send(piece, across) for piece in got]))
        came = came + waiting
        mark = use(sum([c[0] for c in came], []), sum([c[1] for c in came], []))
        last = jnp.concatenate([join(a, mark), b])
        return [(0, far), (1, far)], [last, send(last, across)]

    def where(items):
        return jnp.stack([index(h, i) for h, i in items]).astype(jnp.int32)

    features = basis.shape[0] * 2 * chips
    wire_scale = 2.0 ** math.floor(math.log2(60000.0 / (X_MAX * BASIS_MAX * features)))
    listed = [(h, i) for r in rounds for h in range(2) for i in r]
    x, tiles = start(where(listed), token_ids.reshape(-1, 1), hidden_pool, basis, kb)

    def projected(r):
        first = sum(2 * len(items) for items in rounds[:r])
        return lambda mark: project(first, (len(rounds[r]),) * 2, x, tiles, x if mark is None else mark)

    def rounded(keep, other, to_right, to_left):
        total = (keep[0] + other[0]) * wire_scale + to_right.astype(F32) + to_left.astype(F32)
        return (total * (1.0 / wire_scale)).astype(BF16)

    own = scatter_sum([projected(r) for r in range(far + 1)], F16, wire_scale, rounded)

    state = {"acc": None, "grad": None}

    def use_forward(items, blocks):
        state["acc"], mark = predict(where(items), coeffs, blocks, state["acc"])
        return mark

    items, last = gather(own, use_forward, True)
    res, low, keep, out = residuals(where(items), coeffs, last, targets, state["acc"])

    def backed(r):
        return lambda mark: backward(both(rounds[r]), coeffs, low, keep if mark is None else mark, kb)

    parts = [lambda mark: (keep, out)] + [backed(r) for r in range(1, far + 1)]
    own = scatter_sum(parts, BF16, 1.0, finish)
    xt = x.T

    def use_back(items, blocks):
        state["grad"], mark = gradient(where(items), xt, blocks, state["grad"], rank, -1.0 / tok_count)
        return mark

    use_back(*gather(own, use_back, False))
    return res, state["grad"]


def solution(mesh):
    placed = (
        P("groups", None),
        P("groups", "layer"),
        P("layer", "groups"),
        P(None, "groups", "layer"),
        P("groups", None, "layer"),
    )
    count = mesh.shape["layer"]
    body = functools.partial(staged, 4) if count == 16 else plain
    return jax.shard_map(
        body,
        mesh=mesh,
        in_specs=placed,
        out_specs=(P("groups", None, "layer"), P("layer", "groups")),
        check_vma=False,
    )
```

time: 446 us -> 191 us (0.43)
  blocking collectives: 181 us -> 0 us
  waiting for transfers between devices: 162 us -> 51.6 us
  Pallas kernels: 0 us -> 93.2 us
  matrix products: 77.1 us -> 0 us
  starting transfers between devices: 0.08 us -> 37.2 us
  between operations: 14.1 us -> 1.75 us
    psum x1 -> x0, blocking collectives: 181 us -> none  [on_device(): lax.psum(summed.reshape(rank_total, row_count), 'layer')]
    reduce_scatter x1 -> x0, waiting for transfers between devices: 108 us -> none  [on_device(): lax.psum_scatter(lax.dot_general(basis, x_local, (((0,), (1,)), ((), ()))...]
    pallas_call x0 -> x37, Pallas kernels: none -> 93.2 us  [the longest x4 30 us: backward(): pl.pallas_call(functools.partial(backward_body, n), out_shape=(half, half...]
    dot_general x4 -> x0, matrix products: 77.1 us -> none  [the longest x1 31.5 us: on_device(): jnp.einsum('lko,lso->kls', coeff_part, res_low, preferred_element_type=jn...]
    all_gather x1 -> x0, waiting for transfers between devices: 53.9 us -> none  [on_device(): piece = lax.all_gather(proj_share, 'layer', axis=0, tiled=True)]
    ppermute x0 -> x58, waiting for transfers between devices: none -> 51.6 us  [send(): return lax.ppermute(a, 'layer', pairs)]
    ppermute x0 -> x58, starting transfers between devices: none -> 37.2 us  [send(): return lax.ppermute(a, 'layer', pairs)]
    gather x1 -> x0, local copies, waits for them, and re-layouts: 5.46 us -> none  [on_device(): x_local = jnp.take(hidden_pool, token_ids.reshape(-1), axis=0)]
  transfers between devices with their start and end apart: 2 -> 58, of which waited for: 2 -> 22; matrix products, arithmetic and copies ran while one was open for 0% -> 1% of each run, Pallas kernels for 0% -> 40%
where the time goes in v1:
time: 191 us
  Pallas kernels  93.2 us (49%)
  waiting for transfers between devices  51.6 us (27%)
  starting transfers between devices  37.2 us (19%)
  local copies, waits for them, and re-layouts  3.82 us (2%)
  other arithmetic  3.36 us (2%)
    ppermute x58, waiting for transfers between devices, send(): return lax.ppermute(a, 'layer', pairs)  51.6 us
    ppermute x58, starting transfers between devices, send(): return lax.ppermute(a, 'layer', pairs)  37.2 us
    pallas_call x4, Pallas kernels, backward(): pl.pallas_call(functools.partial(backward_body, n), out_shape=(half, half...  30 us
    pallas_call x4, Pallas kernels, predict(): pl.pallas_call(functools.partial(predict_body, n, first), out_shape=(jax....  26.4 us
    pallas_call x5, Pallas kernels, gradient(): pl.pallas_call(functools.partial(gradient_body, n, scale, first), out_sha...  17.8 us
    pallas_call x1, Pallas kernels, residuals(): pl.pallas_call(functools.partial(residual_body, n), out_shape=(jax.ShapeD...  7.95 us
    pallas_call x5, Pallas kernels, project(): pl.pallas_call(functools.partial(project_body, first, sizes), out_shape=t...  6.67 us
    pallas_call x1, Pallas kernels, start(): pl.pallas_call(functools.partial(start_body, 256, kb), out_shape=(jax.Sha...  4.18 us
  transfers between devices with their start and end apart: 58, of which 22 were waited for; matrix products, arithmetic and copies ran while one was open for 1% of the time, Pallas kernels for 40%

profile of v1, /device:TPU:0, one launch (start us, length us, event | category | flops | bytes accessed | tf_op | source)
XLA Modules:
  0.0 190.9 jit_solution(7443917955379167017)
XLA Ops:
  4.3 4.2 %start.1 = (bf16[512,1024]{1,0:T(8,128)(2,1)S(1)}, bf16[16,1024,256]{2,1,0:T(8,128)(2,1)S(1)}) custom-call(s32[16]{0:T(128)S(1)} %stack.73.idx_ref, bf16[512,2048]{1,0:T(8,128)(2,1)S(1)} %fusion.hot_ref, bf16[2048,1024]{1,0:T(8,128)(2,1)S(1)} %copy-done.2, bf16[1024,4096]{1,0:T(8,128)(2,1)} %basis_ref.1), custom_call_target="tpu_custom_call" | custom-call | flops 2147483648 | bytes 4194304 | tf_op jit(solution)/shard_map/start/pallas_call | solution.py:72
  11.8 3.0 %collective-permute-start.2 = (f16[256,256]{1,0:T(8,128)(2,1)S(1)}, f16[256,256]{1,0:T(8,128)(2,1)S(1)}, u32[]{:S(2)}, u32[]{:S(2)}) collective-permute-start(f16[256,256]{1,0:T(8,128)(2,1)S(1)} %get-tuple-element.99), channel_id=1, source_target_pairs={{0,4},{1,5},{4,8},{5,9},{8,12},{9,13},{12,14},{13,15},{14,10},{15,... | collective-permute-start | bytes 393224 | tf_op jit(solution)/shard_map/ppermute | solution.py:369
  22.9 4.7 %collective-permute-done.4 = f16[512,256]{1,0:T(8,128)(2,1)S(1)} collective-permute-done((f16[512,256]{1,0:T(8,128)(2,1)S(1)}, f16[512,256]{1,0:T(8,128)(2,1)S(1)}, u32[]{:S(2)}, u32[]{:S(2)}) %collective-permute-start.4) | collective-permute-done | bytes 262176 | tf_op jit(solution)/shard_map/ppermute | solution.py:369
  32.4 5.9 %collective-permute-done.11 = f16[512,256]{1,0:T(8,128)(2,1)S(1)} collective-permute-done((f16[512,256]{1,0:T(8,128)(2,1)S(1)}, f16[512,256]{1,0:T(8,128)(2,1)S(1)}, u32[]{:S(2)}, u32[]{:S(2)}) %collective-permute-start.11) | collective-permute-done | bytes 262176 | tf_op jit(solution)/shard_map/ppermute | solution.py:369
  40.8 6.6 %collective-permute-done.12 = f16[512,256]{1,0:T(8,128)(2,1)S(1)} collective-permute-done((f16[512,256]{1,0:T(8,128)(2,1)S(1)}, f16[512,256]{1,0:T(8,128)(2,1)S(1)}, u32[]{:S(2)}, u32[]{:S(2)}) %collective-permute-start.12) | collective-permute-done | bytes 262176 | tf_op jit(solution)/shard_map/ppermute | solution.py:369
  51.2 2.8 %predict.4 = (f32[512,1024]{1,0:T(8,128)S(1)}, f32[8,128]{1,0:T(8,128)S(1)}) custom-call(s32[1]{0:T(128)} %bitcast.14.idx_ref, bf16[8,4096,1024]{2,1,0:T(8,128)(2,1)} %coeff_ref.17, bf16[512,256]{1,0:T(8,128)(2,1)S(1)} %fusion.33.refs_0_), custom_call_target="tpu_custom_call" | custom-call | flops 1073741824 | bytes 4194304 | tf_op jit(solution)/shard_map/predict/pallas_call | solution.py:186
  54.0 2.6 %collective-permute-done.13.value_ref = bf16[512,256]{1,0:T(8,128)(2,1)S(1)} collective-permute-done((bf16[512,256]{1,0:T(8,128)(2,1)S(1)}, bf16[512,256]{1,0:T(8,128)(2,1)S(1)}, u32[]{:S(2)}, u32[]{:S(2)}) %collective-permute-start.13) | collective-permute-done | bytes 262176 | tf_op jit(solution)/shard_map/ppermute | solution.py:369
  59.8 5.7 %predict.5 = (f32[512,1024]{1,0:T(8,128)S(1)}, f32[8,128]{1,0:T(8,128)S(1)}) custom-call(s32[3]{0:T(128)S(1)} %pad_add_fusion.1.idx_ref, bf16[8,4096,1024]{2,1,0:T(8,128)(2,1)} %coeff_ref.17, bf16[512,256]{1,0:T(8,128)(2,1)S(1)} %collective-permute-done.15.refs_0_, bf16[512,256]{1,0:T(8,128)(2,1)S(1)} %join.20.refs_1_, ...), custom_call_target="tpu_custom_call", output_to_operand_aliasing={{0}: (5, {})} | custom-call | flops 3221225472 | bytes 12582912 | tf_op jit(solution)/shard_map/predict/pallas_call | solution.py:186
  68.5 7.4 %predict.6 = (f32[512,1024]{1,0:T(8,128)S(1)}, f32[8,128]{1,0:T(8,128)S(1)}) custom-call(s32[4]{0:T(128)S(1)} %pad_add_fusion.2.idx_ref, bf16[8,4096,1024]{2,1,0:T(8,128)(2,1)} %coeff_ref.17, bf16[512,256]{1,0:T(8,128)(2,1)S(1)} %collective-permute-done.18.refs_0_, ...), custom_call_target="tpu_custom_call", output_to_operand_aliasing={{0}: (6, {})} | custom-call | flops 4294967296 | bytes 16777216 | tf_op jit(solution)/shard_map/predict/pallas_call | solution.py:186
  78.8 10.5 %predict.7 = (f32[512,1024]{1,0:T(8,128)S(1)}, f32[8,128]{1,0:T(8,128)S(1)}) custom-call(s32[6]{0:T(128)S(1)} %stack.152.idx_ref, bf16[8,4096,1024]{2,1,0:T(8,128)(2,1)} %coeff_ref.17, bf16[512,256]{1,0:T(8,128)(2,1)S(1)} %collective-permute-done.22.refs_0_, bf16[512,256]{1,0:T(8,128)(2,1)} %collective-permute-done.23.refs_1_, ...), custom_call_target="tpu_custom_call", output_to_operand_aliasing={{0}: (8, {})} | custom-call | flops 6442450944 | bytes 25165824 | tf_op jit(solution)/shard_map/predict/pallas_call | solution.py:186
  90.9 7.9 %residuals.1 = (f32[8,64,1024]{2,1,0:T(8,128)}, bf16[512,1024]{1,0:T(8,128)(2,1)S(1)}, f32[1,256,512]{2,1,0:T(8,128)S(1)}, f32[1,256,512]{2,1,0:T(8,128)S(1)}) custom-call(s32[2]{0:T(128)S(1)} %pad_add_fusion.idx_ref, bf16[8,4096,1024]{2,1,0:T(8,128)(2,1)} %coeff_ref.17, bf16[512,256]{1,0:T(8,128)(2,1)S(1)} %pad_maximum_fusion.2.refs_0_, ...), custom_call_target="tpu_custom_call" | custom-call | flops 4294967296 | bytes 8388608 | tf_op jit(solution)/shard_map/residuals/pallas_call | solution.py:242
  99.2 8.3 %backward.5 = (f32[2,256,512]{2,1,0:T(8,128)S(1)}, f32[2,256,512]{2,1,0:T(8,128)S(1)}) custom-call(s32[4]{0:T(128)S(1)} %pad_add_fusion.5.idx_ref, bf16[8,4096,1024]{2,1,0:T(8,128)(2,1)} %coeff_ref.17, bf16[512,1024]{1,0:T(8,128)(2,1)S(1)} %get-tuple-element.64.low_ref, f32[1,256,512]{2,1,0:T(8,128)S(1)} %get-tuple-element.65.mark_ref), custom_call_target="tpu_custom_call" | custom-call | flops 4294967296 | bytes 16777216 | tf_op jit(solution)/shard_map/backward/pallas_call | solution.py:278
  110.2 8.3 %backward.4 = (f32[2,256,512]{2,1,0:T(8,128)S(1)}, f32[2,256,512]{2,1,0:T(8,128)S(1)}) custom-call(s32[4]{0:T(128)S(1)} %pad_add_fusion.4.idx_ref, bf16[8,4096,1024]{2,1,0:T(8,128)(2,1)} %coeff_ref.17, bf16[512,1024]{1,0:T(8,128)(2,1)S(1)} %get-tuple-element.64.low_ref, f32[8,128]{1,0:T(8,128)S(1)} %slice_convert_fusion.7.mark_ref), custom_call_target="tpu_custom_call" | custom-call | flops 4294967296 | bytes 16777216 | tf_op jit(solution)/shard_map/backward/pallas_call | solution.py:278
  121.2 8.2 %backward.7 = (f32[2,256,512]{2,1,0:T(8,128)S(1)}, f32[2,256,512]{2,1,0:T(8,128)S(1)}) custom-call(s32[4]{0:T(128)S(1)} %pad_add_fusion.6.idx_ref, bf16[8,4096,1024]{2,1,0:T(8,128)(2,1)} %coeff_ref.17, bf16[512,1024]{1,0:T(8,128)(2,1)S(1)} %get-tuple-element.64.low_ref, f32[8,128]{1,0:T(8,128)S(1)} %slice_convert_fusion.6.mark_ref), custom_call_target="tpu_custom_call" | custom-call | flops 4294967296 | bytes 16777216 | tf_op jit(solution)/shard_map/backward/pallas_call | solution.py:278
  132.0 5.3 %backward.6 = (f32[1,256,512]{2,1,0:T(8,128)S(1)}, f32[1,256,512]{2,1,0:T(8,128)S(1)}) custom-call(s32[2]{0:T(128)S(1)} %pad_add_fusion.3.idx_ref, bf16[8,4096,1024]{2,1,0:T(8,128)(2,1)} %coeff_ref.17, bf16[512,1024]{1,0:T(8,128)(2,1)S(1)} %get-tuple-element.64.low_ref, f32[8,128]{1,0:T(8,128)S(1)} %slice_convert_fusion.5.mark_ref), custom_call_target="tpu_custom_call" | custom-call | flops 2147483648 | bytes 8388608 | tf_op jit(solution)/shard_map/backward/pallas_call | solution.py:278
  141.3 6.6 %collective-permute-done.37.right_ref = bf16[256,512]{1,0:T(8,128)(2,1)S(1)} collective-permute-done((bf16[256,512]{1,0:T(8,128)(2,1)S(1)}, bf16[256,512]{1,0:T(8,128)(2,1)S(1)}, u32[]{:S(2)}, u32[]{:S(2)}) %collective-permute-start.37) | collective-permute-done | bytes 262176 | tf_op jit(solution)/shard_map/ppermute | solution.py:369
  152.3 2.7 %gradient.5 = (f32[1024,4096]{1,0:T(8,128)}, f32[8,128]{1,0:T(8,128)S(1)}) custom-call(s32[2]{0:T(128)S(1)} %pad_add_fusion.3.idx_ref, bf16[1024,512]{1,0:T(8,128)(2,1)S(1)} %bitcast.115, bf16[512,256]{1,0:T(8,128)(2,1)S(1)} %finish.1.refs_0_, bf16[512,256]{1,0:T(8,128)(2,1)S(1)} %collective-permute-done.43.refs_1_), custom_call_target="tpu_custom_call" | custom-call | flops 536870912 | bytes 2097152 | tf_op jit(solution)/shard_map/gradient/pallas_call | solution.py:316
  155.0 3.4 %collective-permute-done.42.value_ref = bf16[512,256]{1,0:T(8,128)(2,1)S(1)} collective-permute-done((bf16[512,256]{1,0:T(8,128)(2,1)S(1)}, bf16[512,256]{1,0:T(8,128)(2,1)S(1)}, u32[]{:S(2)}, u32[]{:S(2)}) %collective-permute-start.42) | collective-permute-done | bytes 262176 | tf_op jit(solution)/shard_map/ppermute | solution.py:369
  161.5 3.9 %gradient.6 = (f32[1024,4096]{1,0:T(8,128)}, f32[8,128]{1,0:T(8,128)S(1)}) custom-call(s32[4]{0:T(128)S(1)} %pad_add_fusion.7.idx_ref, bf16[1024,512]{1,0:T(8,128)(2,1)S(1)} %bitcast.116, bf16[512,256]{1,0:T(8,128)(2,1)S(1)} %join.28.refs_0_, bf16[512,256]{1,0:T(8,128)(2,1)S(1)} %collective-permute-done.45.refs_1_, ...), custom_call_target="tpu_custom_call", output_to_operand_aliasing={{0}: (6, {})} | custom-call | flops 1073741824 | bytes 4194304 | tf_op jit(solution)/shard_map/gradient/pallas_call | solution.py:316
  165.4 2.7 %collective-permute-done.44.value_ref = bf16[512,256]{1,0:T(8,128)(2,1)S(1)} collective-permute-done((bf16[512,256]{1,0:T(8,128)(2,1)S(1)}, bf16[512,256]{1,0:T(8,128)(2,1)S(1)}, u32[]{:S(2)}, u32[]{:S(2)}) %collective-permute-start.44) | collective-permute-done | bytes 262176 | tf_op jit(solution)/shard_map/ppermute | solution.py:369
  171.5 3.9 %gradient.7 = (f32[1024,4096]{1,0:T(8,128)}, f32[8,128]{1,0:T(8,128)S(1)}) custom-call(s32[4]{0:T(128)S(1)} %pad_add_fusion.8.idx_ref, bf16[1024,512]{1,0:T(8,128)(2,1)S(1)} %bitcast.117, bf16[512,256]{1,0:T(8,128)(2,1)S(1)} %join.29.refs_0_, bf16[512,256]{1,0:T(8,128)(2,1)S(1)} %collective-permute-done.49.refs_1_, ...), custom_call_target="tpu_custom_call", output_to_operand_aliasing={{0}: (6, {})} | custom-call | flops 1073741824 | bytes 4194304 | tf_op jit(solution)/shard_map/gradient/pallas_call | solution.py:316
  175.5 2.7 %collective-permute-done.48.value_ref = bf16[512,256]{1,0:T(8,128)(2,1)S(1)} collective-permute-done((bf16[512,256]{1,0:T(8,128)(2,1)S(1)}, bf16[512,256]{1,0:T(8,128)(2,1)S(1)}, u32[]{:S(2)}, u32[]{:S(2)}) %collective-permute-start.48) | collective-permute-done | bytes 262176 | tf_op jit(solution)/shard_map/ppermute | solution.py:369
  181.6 3.9 %gradient.8 = (f32[1024,4096]{1,0:T(8,128)}, f32[8,128]{1,0:T(8,128)S(1)}) custom-call(s32[4]{0:T(128)S(1)} %pad_add_fusion.9.idx_ref, bf16[1024,512]{1,0:T(8,128)(2,1)S(1)} %bitcast.118, bf16[512,256]{1,0:T(8,128)(2,1)S(1)} %join.30.refs_0_, bf16[512,256]{1,0:T(8,128)(2,1)S(1)} %collective-permute-done.53.refs_1_, ...), custom_call_target="tpu_custom_call", output_to_operand_aliasing={{0}: (6, {})} | custom-call | flops 1073741824 | bytes 4194304 | tf_op jit(solution)/shard_map/gradient/pallas_call | solution.py:316
  187.5 3.3 %gradient.9 = (f32[1024,4096]{1,0:T(8,128)}, f32[8,128]{1,0:T(8,128)}) custom-call(s32[2]{0:T(128)S(1)} %pad_add_fusion.idx_ref, bf16[1024,512]{1,0:T(8,128)(2,1)S(1)} %bitcast.119, bf16[512,256]{1,0:T(8,128)(2,1)S(1)} %pad_maximum_fusion.5.refs_0_, bf16[512,256]{1,0:T(8,128)(2,1)S(1)} %collective-permute-done.57.refs_1_, ...), custom_call_target="tpu_custom_call", output_to_operand_aliasing={{0}: (4, {})} | custom-call | flops 536870912 | bytes 2097152 | tf_op jit(solution)/shard_map/gradient/pallas_call | solution.py:316
  (189 shorter events, 64.7 us)
Async XLA Ops:
  18.7 10.7 %collective-permute-start.3 = (f32[2,512,256]{2,1,0:T(8,128)S(1)}, f32[2,512,256]{2,1,0:T(8,128)S(1)}, u32[]{:S(2)}, u32[]{:S(2)}) collective-permute-start(f32[2,512,256]{2,1,0:T(8,128)S(1)} %join.17), channel_id=1, source_target_pairs={{0,1},{1,0},{2,3},{3,2},{4,5},{5,4},{6,7},{7,6},{8,9},{9,8},{10,11... | collective-permute-start | bytes 3145736 | tf_op jit(solution)/shard_map/ppermute | solution.py:369
  18.8 8.8 %collective-permute-start.4 = (f16[512,256]{1,0:T(8,128)(2,1)S(1)}, f16[512,256]{1,0:T(8,128)(2,1)S(1)}, u32[]{:S(2)}, u32[]{:S(2)}) collective-permute-start(f16[512,256]{1,0:T(8,128)(2,1)S(1)} %pad_maximum_fusion), channel_id=1, source_target_pairs={{0,4},{1,5},{4,8},{5,9},{8,12},{9,13},{12,14},{13,15},{14,10},{15,... | collective-permute-start | bytes 786440 | tf_op jit(solution)/shard_map/ppermute | solution.py:369
  29.6 8.8 %collective-permute-start.5 = (f32[2,512,256]{2,1,0:T(8,128)S(1)}, f32[2,512,256]{2,1,0:T(8,128)S(1)}, u32[]{:S(2)}, u32[]{:S(2)}) collective-permute-start(f32[2,512,256]{2,1,0:T(8,128)S(1)} %join.18), channel_id=1, source_target_pairs={{0,1},{1,0},{2,3},{3,2},{4,5},{5,4},{6,7},{7,6},{8,9},{9,8},{10,11... | collective-permute-start | bytes 3145736 | tf_op jit(solution)/shard_map/ppermute | solution.py:369
  38.6 10.2 %collective-permute-start.7 = (f32[1,512,256]{2,1,0:T(8,128)S(1)}, f32[1,512,256]{2,1,0:T(8,128)S(1)}, u32[]{:S(2)}, u32[]{:S(2)}) collective-permute-start(f32[1,512,256]{2,1,0:T(8,128)S(1)} %join.19), channel_id=1, source_target_pairs={{0,1},{1,0},{2,3},{3,2},{4,5},{5,4},{6,7},{7,6},{8,9},{9,8},{10,11... | collective-permute-start | bytes 1572872 | tf_op jit(solution)/shard_map/ppermute | solution.py:369
  49.4 10.4 %collective-permute-start.15 = (bf16[512,256]{1,0:T(8,128)(2,1)S(1)}, bf16[512,256]{1,0:T(8,128)(2,1)S(1)}, u32[]{:S(2)}, u32[]{:S(2)}) collective-permute-start(bf16[512,256]{1,0:T(8,128)(2,1)S(1)} %fusion.33.refs_0_), channel_id=1, source_target_pairs={{0,1},{1,0},{2,3},{3,2},{4,5},{5,4},{6,7},{7,6},{8,9},{9,8},{10,11... | collective-permute-start | bytes 786440 | tf_op jit(solution)/shard_map/ppermute | solution.py:369
  49.4 8.7 %collective-permute-start.16 = (bf16[512,256]{1,0:T(8,128)(2,1)S(1)}, bf16[512,256]{1,0:T(8,128)(2,1)S(1)}, u32[]{:S(2)}, u32[]{:S(2)}) collective-permute-start(bf16[512,256]{1,0:T(8,128)(2,1)S(1)} %fusion.33.refs_0_), channel_id=1, source_target_pairs={{0,2},{1,3},{4,0},{5,1},{8,4},{9,5},{12,8},{13,9},{14,12},{15,13},... | collective-permute-start | bytes 786440 | tf_op jit(solution)/shard_map/ppermute | solution.py:369
  56.6 9.0 %collective-permute-start.14 = (bf16[512,256]{1,0:T(8,128)(2,1)S(1)}, bf16[512,256]{1,0:T(8,128)(2,1)S(1)}, u32[]{:S(2)}, u32[]{:S(2)}) collective-permute-start(bf16[512,256]{1,0:T(8,128)(2,1)S(1)} %join.20.refs_1_), channel_id=1, source_target_pairs={{0,4},{1,5},{4,8},{5,9},{8,12},{9,13},{12,14},{13,15},{14,10},{15,... | collective-permute-start | bytes 786440 | tf_op jit(solution)/shard_map/ppermute | solution.py:369
  57.3 11.3 %collective-permute-start.18 = (bf16[512,256]{1,0:T(8,128)(2,1)S(1)}, bf16[512,256]{1,0:T(8,128)(2,1)S(1)}, u32[]{:S(2)}, u32[]{:S(2)}) collective-permute-start(bf16[512,256]{1,0:T(8,128)(2,1)S(1)} %join.20.refs_1_), channel_id=1, source_target_pairs={{0,1},{1,0},{2,3},{3,2},{4,5},{5,4},{6,7},{7,6},{8,9},{9,8},{10,11... | collective-permute-start | bytes 786440 | tf_op jit(solution)/shard_map/ppermute | solution.py:369
  58.1 10.4 %collective-permute-start.19 = (bf16[512,256]{1,0:T(8,128)(2,1)S(1)}, bf16[512,256]{1,0:T(8,128)(2,1)S(1)}, u32[]{:S(2)}, u32[]{:S(2)}) collective-permute-start(bf16[512,256]{1,0:T(8,128)(2,1)S(1)} %collective-permute-done.16.refs_2_), channel_id=1, source_target_pairs={{0,1},{1,0},{2,3},{3,2},{4,5},{5,4},{6,7},{7,6},{8,9},{9,8},{10,11... | collective-permute-start | bytes 786440 | tf_op jit(solution)/shard_map/ppermute | solution.py:369
  58.1 8.7 %collective-permute-start.20 = (bf16[512,256]{1,0:T(8,128)(2,1)S(1)}, bf16[512,256]{1,0:T(8,128)(2,1)S(1)}, u32[]{:S(2)}, u32[]{:S(2)}) collective-permute-start(bf16[512,256]{1,0:T(8,128)(2,1)S(1)} %collective-permute-done.16.refs_2_), channel_id=1, source_target_pairs={{0,2},{1,3},{4,0},{5,1},{8,4},{9,5},{12,8},{13,9},{14,12},{15,13},... | collective-permute-start | bytes 786440 | tf_op jit(solution)/shard_map/ppermute | solution.py:369
  65.6 10.3 %collective-permute-start.17 = (bf16[512,256]{1,0:T(8,128)(2,1)S(1)}, bf16[512,256]{1,0:T(8,128)(2,1)S(1)}, u32[]{:S(2)}, u32[]{:S(2)}) collective-permute-start(bf16[512,256]{1,0:T(8,128)(2,1)S(1)} %join.21.refs_2_), channel_id=1, source_target_pairs={{0,4},{1,5},{4,8},{5,9},{8,12},{9,13},{12,14},{13,15},{14,10},{15,... | collective-permute-start | bytes 786440 | tf_op jit(solution)/shard_map/ppermute | solution.py:369
  66.0 10.9 %collective-permute-start.22 = (bf16[512,256]{1,0:T(8,128)(2,1)S(1)}, bf16[512,256]{1,0:T(8,128)(2,1)S(1)}, u32[]{:S(2)}, u32[]{:S(2)}) collective-permute-start(bf16[512,256]{1,0:T(8,128)(2,1)S(1)} %join.21.refs_2_), channel_id=1, source_target_pairs={{0,1},{1,0},{2,3},{3,2},{4,5},{5,4},{6,7},{7,6},{8,9},{9,8},{10,11... | collective-permute-start | bytes 786440 | tf_op jit(solution)/shard_map/ppermute | solution.py:369
  66.8 9.6 %collective-permute-start.24 = (bf16[512,256]{1,0:T(8,128)(2,1)S(1)}, bf16[512,256]{1,0:T(8,128)(2,1)S(1)}, u32[]{:S(2)}, u32[]{:S(2)}) collective-permute-start(bf16[512,256]{1,0:T(8,128)(2,1)S(1)} %collective-permute-done.20.refs_3_), channel_id=1, source_target_pairs={{0,2},{1,3},{4,0},{5,1},{8,4},{9,5},{12,8},{13,9},{14,12},{15,13},... | collective-permute-start | bytes 786440 | tf_op jit(solution)/shard_map/ppermute | solution.py:369
  68.5 10.2 %collective-permute-start.23 = (bf16[512,256]{1,0:T(8,128)(2,1)S(1)}, bf16[512,256]{1,0:T(8,128)(2,1)}, u32[]{:S(2)}, u32[]{:S(2)}) collective-permute-start(bf16[512,256]{1,0:T(8,128)(2,1)S(1)} %collective-permute-done.20.refs_3_), channel_id=1, source_target_pairs={{0,1},{1,0},{2,3},{3,2},{4,5},{5,4},{6,7},{7,6},{8,9},{9,8},{10,11... | collective-permute-start | bytes 786440 | tf_op jit(solution)/shard_map/ppermute | solution.py:369
  76.6 12.7 %collective-permute-start.21 = (bf16[256,256]{1,0:T(8,128)(2,1)S(1)}, bf16[256,256]{1,0:T(8,128)(2,1)S(1)}, u32[]{:S(2)}, u32[]{:S(2)}) collective-permute-start(bf16[256,256]{1,0:T(8,128)(2,1)S(1)} %slice.262), channel_id=1, source_target_pairs={{0,4},{1,5},{4,8},{5,9},{8,12},{9,13},{12,14},{13,15},{14,10},{15,... | collective-permute-start | bytes 393224 | tf_op jit(solution)/shard_map/ppermute | solution.py:369
  76.9 12.3 %collective-permute-start.27 = (bf16[256,256]{1,0:T(8,128)(2,1)S(1)}, bf16[256,256]{1,0:T(8,128)(2,1)S(1)}, u32[]{:S(2)}, u32[]{:S(2)}) collective-permute-start(bf16[256,256]{1,0:T(8,128)(2,1)S(1)} %slice.263), channel_id=1, source_target_pairs={{0,2},{1,3},{4,0},{5,1},{8,4},{9,5},{12,8},{13,9},{14,12},{15,13},... | collective-permute-start | bytes 393224 | tf_op jit(solution)/shard_map/ppermute | solution.py:369
  107.5 11.0 %collective-permute-start.30 = (f32[2,256,512]{2,1,0:T(8,128)S(1)}, f32[2,256,512]{2,1,0:T(8,128)S(1)}, u32[]{:S(2)}, u32[]{:S(2)}) collective-permute-start(f32[2,256,512]{2,1,0:T(8,128)S(1)} %join.24), channel_id=1, source_target_pairs={{0,1},{1,0},{2,3},{3,2},{4,5},{5,4},{6,7},{7,6},{8,9},{9,8},{10,11... | collective-permute-start | bytes 3145736 | tf_op jit(solution)/shard_map/ppermute | solution.py:369
  108.2 10.6 %collective-permute-start.31 = (bf16[128,512]{1,0:T(8,128)(2,1)S(1)}, bf16[128,512]{1,0:T(8,128)(2,1)S(1)}, u32[]{:S(2)}, u32[]{:S(2)}) collective-permute-start(bf16[128,512]{1,0:T(8,128)(2,1)S(1)} %get-tuple-element.97), channel_id=1, source_target_pairs={{0,4},{1,5},{4,8},{5,9},{8,12},{9,13},{12,14},{13,15},{14,10},{15,... | collective-permute-start | bytes 393224 | tf_op jit(solution)/shard_map/ppermute | solution.py:369
  108.5 10.8 %collective-permute-start.38 = (bf16[128,512]{1,0:T(8,128)(2,1)S(1)}, bf16[128,512]{1,0:T(8,128)(2,1)S(1)}, u32[]{:S(2)}, u32[]{:S(2)}) collective-permute-start(bf16[128,512]{1,0:T(8,128)(2,1)S(1)} %get-tuple-element.96), channel_id=1, source_target_pairs={{0,2},{1,3},{4,0},{5,1},{8,4},{9,5},{12,8},{13,9},{14,12},{15,13},... | collective-permute-start | bytes 393224 | tf_op jit(solution)/shard_map/ppermute | solution.py:369
  118.8 10.6 %collective-permute-start.32 = (f32[2,256,512]{2,1,0:T(8,128)S(1)}, f32[2,256,512]{2,1,0:T(8,128)S(1)}, u32[]{:S(2)}, u32[]{:S(2)}) collective-permute-start(f32[2,256,512]{2,1,0:T(8,128)S(1)} %join.25), channel_id=1, source_target_pairs={{0,1},{1,0},{2,3},{3,2},{4,5},{5,4},{6,7},{7,6},{8,9},{9,8},{10,11... | collective-permute-start | bytes 3145736 | tf_op jit(solution)/shard_map/ppermute | solution.py:369
  118.9 10.5 %collective-permute-start.33 = (bf16[256,512]{1,0:T(8,128)(2,1)S(1)}, bf16[256,512]{1,0:T(8,128)(2,1)S(1)}, u32[]{:S(2)}, u32[]{:S(2)}) collective-permute-start(bf16[256,512]{1,0:T(8,128)(2,1)S(1)} %pad_maximum_fusion.3), channel_id=1, source_target_pairs={{0,4},{1,5},{4,8},{5,9},{8,12},{9,13},{12,14},{13,15},{14,10},{15,... | collective-permute-start | bytes 786440 | tf_op jit(solution)/shard_map/ppermute | solution.py:369
  119.4 10.1 %collective-permute-start.39 = (bf16[256,512]{1,0:T(8,128)(2,1)S(1)}, bf16[256,512]{1,0:T(8,128)(2,1)S(1)}, u32[]{:S(2)}, u32[]{:S(2)}) collective-permute-start(bf16[256,512]{1,0:T(8,128)(2,1)S(1)} %pad_maximum_fusion.4), channel_id=1, source_target_pairs={{0,2},{1,3},{4,0},{5,1},{8,4},{9,5},{12,8},{13,9},{14,12},{15,13},... | collective-permute-start | bytes 786440 | tf_op jit(solution)/shard_map/ppermute | solution.py:369
  129.8 9.0 %collective-permute-start.34 = (f32[2,256,512]{2,1,0:T(8,128)S(1)}, f32[2,256,512]{2,1,0:T(8,128)S(1)}, u32[]{:S(2)}, u32[]{:S(2)}) collective-permute-start(f32[2,256,512]{2,1,0:T(8,128)S(1)} %join.26), channel_id=1, source_target_pairs={{0,1},{1,0},{2,3},{3,2},{4,5},{5,4},{6,7},{7,6},{8,9},{9,8},{10,11... | collective-permute-start | bytes 3145736 | tf_op jit(solution)/shard_map/ppermute | solution.py:369
  139.1 10.3 %collective-permute-start.36 = (f32[1,256,512]{2,1,0:T(8,128)S(1)}, f32[1,256,512]{2,1,0:T(8,128)S(1)}, u32[]{:S(2)}, u32[]{:S(2)}) collective-permute-start(f32[1,256,512]{2,1,0:T(8,128)S(1)} %join.27), channel_id=1, source_target_pairs={{0,1},{1,0},{2,3},{3,2},{4,5},{5,4},{6,7},{7,6},{8,9},{9,8},{10,11... | collective-permute-start | bytes 1572872 | tf_op jit(solution)/shard_map/ppermute | solution.py:369
  (38 other events, 255.8 us)

commit v2 on v1

--- a/solution.py
+++ b/solution.py
@@ -153,8 +153,20 @@
     return jnp.concatenate([piece[span, :] for piece in pieces], axis=1)
 
 
-def predict_body(n, first, idx_ref, coeff_ref, *refs):
-    pieces, rest = refs[:n], refs[n:]
+def predicted(l, span, pieces, copied, buf, held, held_refs):
+    total = None
+    if copied:
+        total = jnp.dot(wide(pieces[:copied], span), buf[l], preferred_element_type=F32)
+    for k in range(held):
+        pair = pieces[copied + 2 * k : copied + 2 * k + 2]
+        part = jnp.dot(wide(pair, span), held_refs[k][l], preferred_element_type=F32)
+        total = part if total is None else total + part
+    return total
+
+
+def predict_body(n, held, first, idx_ref, coeff_ref, *refs):
+    count = n + 2 * held
+    pieces, held_refs, rest = refs[:count], refs[count : count + held], refs[count + held :]
     if first:
         out_ref, mark_ref, buf, sems = rest
     else:
@@ -169,7 +181,7 @@
     def _(l):
         span = rows_of(l, toks)
         wait_coeffs(idx_ref, coeff_ref, buf, sems, n, kb, l)
-        part = jnp.dot(wide(pieces, span), buf[l], preferred_element_type=F32)
+        part = predicted(l, span, pieces, n, buf, held, held_refs)
         out_ref[span, :] = part if first else acc_ref[span, :] + part
 
 
@@ -178,29 +190,58 @@
     return [pltpu.VMEM((layer_count, n * kb, width), BF16), pltpu.SemaphoreType.DMA((layer_count, n))]
 
 
-def predict(idx, coeffs, pieces, acc):
-    n = len(pieces)
+def predict(idx, coeffs, pieces, tiles, acc):
+    n = idx.shape[0]
+    held = len(tiles)
     rows, kb = pieces[0].shape
     layer_count, _, width = coeffs.shape
     first = acc is None
-    return pl.pallas_call(
-        functools.partial(predict_body, n, first),
+    inputs = len(pieces) + held
+    return pl.pallas_call(
+        functools.partial(predict_body, n, held, first),
         out_shape=(jax.ShapeDtypeStruct((rows, width), F32), jax.ShapeDtypeStruct((8, 128), F32)),
-        in_specs=[IN_SMEM, IN_HBM] + [IN_VMEM] * (n + (not first)),
+        in_specs=[IN_SMEM, IN_HBM] + [IN_VMEM] * (inputs + (not first)),
         out_specs=(IN_VMEM, IN_VMEM),
-        input_output_aliases={} if first else {n + 2: 0},
+        input_output_aliases={} if first else {inputs + 2: 0},
         scratch_shapes=coeff_scratch(coeffs, n, kb),
         compiler_params=params(4 * n + 3),
-        cost_estimate=cost(8 * n * rows * kb * width, layer_count * n * kb * width * 2),
+        cost_estimate=cost(8 * len(pieces) * rows * kb * width, layer_count * n * kb * width * 2),
         name="predict",
-    )(idx, coeffs, *pieces, *([] if first else [acc]))
-
-
-def back_blocks(low, buf, l, keep_ref, send_ref, toks):
-    m, kb, _ = keep_ref.shape
+    )(idx, coeffs, *pieces, *tiles, *([] if first else [acc]))
+
+
+def hold_body(n, kb, idx_ref, coeff_ref, after_ref, tiles_ref, mark_ref, sems):
+    mark_ref[...] = jnp.zeros_like(mark_ref)
+    start_coeffs(idx_ref, coeff_ref, tiles_ref, sems, n, kb)
+
+    @pl.loop(0, tiles_ref.shape[0])
+    def _(l):
+        wait_coeffs(idx_ref, coeff_ref, tiles_ref, sems, n, kb, l)
+
+
+def hold(idx, coeffs, kb, mark):
+    n = idx.shape[0]
+    layer_count, _, width = coeffs.shape
+    return pl.pallas_call(
+        functools.partial(hold_body, n, kb),
+        out_shape=(
+            jax.ShapeDtypeStruct((layer_count, n * kb, width), BF16),
+            jax.ShapeDtypeStruct((8, 128), F32),
+        ),
+        in_specs=[IN_SMEM, IN_HBM, IN_VMEM],
+        out_specs=(IN_VMEM, IN_VMEM),
+        scratch_shapes=coeff_scratch(coeffs, n, kb)[1:],
+        compiler_params=params(12),
+        cost_estimate=cost(0, layer_count * n * kb * width * 2),
+        name="hold",
+    )(idx, coeffs, mark)
+
+
+def back_blocks(low, tiles, l, outs, toks):
+    kb = outs[0].shape[0]
     parts = [
         lax.dot_general(
-            buf[l + j],
+            tiles[l + j],
             low[j * toks : (j + 1) * toks, :],
             (((1,), (1,)), ((), ())),
             preferred_element_type=F32,
@@ -209,56 +250,48 @@
     ]
     both = jnp.concatenate(parts, axis=1)
     lanes = pl.ds(pl.multiple_of(l * toks, 2 * toks), 2 * toks)
-    for i in range(m):
-        keep_ref[i, :, lanes] = both[i * kb : (i + 1) * kb, :]
-        send_ref[i, :, lanes] = both[(m + i) * kb : (m + i + 1) * kb, :]
-
-
-def residual_body(n, idx_ref, coeff_ref, *refs):
-    pieces, (target_ref, acc_ref, res_ref, low_ref, keep_ref, send_ref, buf, sems) = refs[:n], refs[n:]
-    layer_count = buf.shape[0]
-    rows, kb = pieces[0].shape
-    toks = rows // layer_count
-    start_coeffs(idx_ref, coeff_ref, buf, sems, n, kb)
+    for i, out in enumerate(outs):
+        out[:, lanes] = both[i * kb : (i + 1) * kb, :]
+
+
+def residual_body(a_ref, b_ref, tiles_ref, target_ref, acc_ref, res_ref, low_ref, keep_ref, send_ref):
+    layer_count, toks, _ = target_ref.shape
 
     @pl.loop(0, layer_count, step=2)
     def _(l):
         for j in range(2):
             span = rows_of(l + j, toks)
-            wait_coeffs(idx_ref, coeff_ref, buf, sems, n, kb, l + j)
-            part = jnp.dot(wide(pieces, span), buf[l + j], preferred_element_type=F32)
+            part = predicted(l + j, span, (a_ref, b_ref), 0, None, 1, (tiles_ref,))
             res = target_ref[l + j].astype(F32) - (acc_ref[span, :] + part)
             res_ref[l + j] = res
             low_ref[span, :] = res.astype(BF16)
         pair = pl.ds(pl.multiple_of(l * toks, 2 * toks), 2 * toks)
-        back_blocks(low_ref[pair, :], buf, l, keep_ref, send_ref, toks)
-
-
-def residuals(idx, coeffs, pieces, targets, acc):
-    n = len(pieces)
+        back_blocks(low_ref[pair, :], tiles_ref, l, [keep_ref.at[0], send_ref.at[0]], toks)
+
+
+def residuals(pieces, tiles, targets, acc):
     rows, kb = pieces[0].shape
-    layer_count, _, width = coeffs.shape
-    half = jax.ShapeDtypeStruct((n // 2, kb, rows), F32)
-    return pl.pallas_call(
-        functools.partial(residual_body, n),
+    layer_count, _, width = targets.shape
+    half = jax.ShapeDtypeStruct((1, kb, rows), F32)
+    return pl.pallas_call(
+        residual_body,
         out_shape=(
             jax.ShapeDtypeStruct(targets.shape, F32),
             jax.ShapeDtypeStruct((rows, width), BF16),
             half,
             half,
         ),
-        in_specs=[IN_SMEM, IN_HBM] + [IN_VMEM] * (n + 2),
+        in_specs=[IN_VMEM] * 5,
         out_specs=(IN_VMEM,) * 4,
-        scratch_shapes=coeff_scratch(coeffs, n, kb),
-        compiler_params=params(4 * n + 3),
-        cost_estimate=cost(16 * n * rows * kb * width, layer_count * n * kb * width * 2),
+        compiler_params=params(8),
+        cost_estimate=cost(32 * rows * kb * width, tiles.size * 2),
         name="residuals",
-    )(idx, coeffs, *pieces, targets, acc)
+    )(*pieces, tiles, targets, acc)
 
 
 def backward_body(n, idx_ref, coeff_ref, low_ref, mark_ref, keep_ref, send_ref, buf, sems):
     layer_count = buf.shape[0]
-    kb = keep_ref.shape[1]
+    m, kb, _ = keep_ref.shape
     toks = low_ref.shape[0] // layer_count
     start_coeffs(idx_ref, coeff_ref, buf, sems, n, kb)
 
@@ -267,7 +300,8 @@
         for j in range(2):
             wait_coeffs(idx_ref, coeff_ref, buf, sems, n, kb, l + j)
         pair = pl.ds(pl.multiple_of(l * toks, 2 * toks), 2 * toks)
-        back_blocks(low_ref[pair, :], buf, l, keep_ref, send_ref, toks)
+        outs = [keep_ref.at[i] for i in range(m)] + [send_ref.at[i] for i in range(m)]
+        back_blocks(low_ref[pair, :], buf, l, outs, toks)
 
 
 def backward(idx, coeffs, low, mark, kb):
@@ -285,6 +319,33 @@
         cost_estimate=cost(8 * n * rows * kb * width, layer_count * n * kb * width * 2),
         name="backward",
     )(idx, coeffs, low, mark)
+
+
+def backward_held_body(layer_count, low_ref, mark_ref, *refs):
+    tiles, (keep_ref, send_ref) = refs[:-2], refs[-2:]
+    toks = low_ref.shape[0] // layer_count
+
+    @pl.loop(0, layer_count, step=2)
+    def _(l):
+        pair = pl.ds(pl.multiple_of(l * toks, 2 * toks), 2 * toks)
+        for i, tile in enumerate(tiles):
+            back_blocks(low_ref[pair, :], tile, l, [keep_ref.at[i], send_ref.at[i]], toks)
+
+
+def backward_held(tiles, low, mark, kb):
+    m = len(tiles)
+    rows = low.shape[0]
+    layer_count, _, width = tiles[0].shape
+    half = jax.ShapeDtypeStruct((m, kb, rows), F32)
+    return pl.pallas_call(
+        functools.partial(backward_held_body, layer_count),
+        out_shape=(half, half),
+        in_specs=[IN_VMEM] * (m + 2),
+        out_specs=(IN_VMEM,) * 2,
+        compiler_params=params(8),
+        cost_estimate=cost(16 * m * rows * kb * width, m * tiles[0].size * 2),
+        name="backward_held",
+    )(low, mark, *tiles)
 
 
 def gradient_body(n, scale, first, idx_ref, xt_ref, *refs):
@@ -377,32 +438,40 @@
     def both(items):
         return jnp.stack([index(h, i) for h in range(2) for i in items]).astype(jnp.int32)
 
-    def scatter_sum(parts, wire, scale, last):
-        keeps, others = [], []
+    def scatter_sum(parts, wire, scale, last, ahead=None):
+        keeps = [[] for _ in parts]
+        others = [[] for _ in parts]
+
+        def compute(r, mark, part=None):
+            keep, out = (part or parts[r])(mark)
+            keeps[r].append(keep)
+            return out
+
+        def swap(r, out, mark=None):
+            others[r].append(send(out if mark is None else join(out, mark), across))
 
         def mine(r, j):
-            return (keeps[r][j] + others[r][j]) * scale
-
-        def blocks(r, mark):
-            keep, out = parts[r](mark)
-            keeps.append(keep)
-            return out
-
-        def swap(out, mark):
-            others.append(send(out if mark is None else join(out, mark), across))
+            at = [(k, i) for k, a in enumerate(keeps[r]) for i in range(a.shape[0])][j]
+            return (keeps[r][at[0]][at[1]] + others[r][at[0]][at[1]]) * scale
 
         def corner(message):
             return message[:8, :128].astype(F32)
 
-        swap(blocks(0, None), None)
-        out = blocks(1, None)
+        swap(0, compute(0, None))
+        split = parts[1] if isinstance(parts[1], list) else [parts[1]]
+        out = compute(1, keeps[0][0], split[0])
         first = mine(0, 0).astype(wire)
         cut = first.shape[0] // 2
         to_right, to_left = send(first[:cut], right), send(first[cut:], left)
         for r in range(1, far):
             mark = corner(first)
-            swap(out, mark)
-            out = blocks(r + 1, mark)
+            swap(r, out, mark)
+            if r == 1 and len(split) > 1:
+                swap(r, compute(r, mark, split[1]))
+                mark = keeps[r][1]
+            if ahead is not None and r >= 2:
+                mark = ahead(r - 2, mark)
+            out = compute(r + 1, mark)
             a, b = mine(r, 0), mine(r, 1)
             if r == 1:
                 a = jnp.concatenate([a[:cut] + to_right.astype(F32), a[cut:]])
@@ -411,8 +480,9 @@
                 a, b = a + to_right.astype(F32), b + to_left.astype(F32)
             first, second = a.astype(wire), b.astype(wire)
             to_right, to_left = send(first, right), send(second, left)
-        swap(out, corner(first))
-        return last(keeps[far], others[far], to_right, to_left)
+        mark = corner(first)
+        swap(far, out, mark)
+        return last(keeps[far][0], others[far][0], to_right, to_left)
 
     def gather(own, use, lag):
         a, b = send(own, right), send(own, left)
@@ -453,21 +523,41 @@
         total = (keep[0] + other[0]) * wire_scale + to_right.astype(F32) + to_left.astype(F32)
         return (total * (1.0 / wire_scale)).astype(BF16)
 
-    own = scatter_sum([projected(r) for r in range(far + 1)], F16, wire_scale, rounded)
+    kept = [far] + rounds[1]
+    held = {}
+
+    def ahead(r, mark):
+        if r >= len(kept):
+            return mark
+        held[kept[r]], mark = hold(where([(0, kept[r]), (1, kept[r])]), coeffs, kb, mark)
+        return mark
+
+    own = scatter_sum([projected(r) for r in range(far + 1)], F16, wire_scale, rounded, ahead)
 
     state = {"acc": None, "grad": None}
 
     def use_forward(items, blocks):
-        state["acc"], mark = predict(where(items), coeffs, blocks, state["acc"])
+        found = dict(zip(items, blocks))
+        near = [item for item in items if item[1] not in held]
+        pairs = [i for i in kept if (0, i) in found and (1, i) in found]
+        ordered = [found[item] for item in near] + [found[h, i] for i in pairs for h in range(2)]
+        assert len(ordered) == len(items)
+        state["acc"], mark = predict(where(near), coeffs, ordered, [held[i] for i in pairs], state["acc"])
+        if len(held) < len(kept):
+            mark = ahead(len(held), mark)
         return mark
 
     items, last = gather(own, use_forward, True)
-    res, low, keep, out = residuals(where(items), coeffs, last, targets, state["acc"])
+    res, low, keep, out = residuals(last, held[far], targets, state["acc"])
 
     def backed(r):
-        return lambda mark: backward(both(rounds[r]), coeffs, low, keep if mark is None else mark, kb)
-
-    parts = [lambda mark: (keep, out)] + [backed(r) for r in range(1, far + 1)]
+        return lambda mark: backward(both(rounds[r]), coeffs, low, mark, kb)
+
+    parts = [
+        lambda mark: (keep, out),
+        [lambda mark, i=i: backward_held([held[i]], low, mark, kb) for i in rounds[1]],
+    ]
+    parts += [backed(r) for r in range(2, far + 1)]
     own = scatter_sum(parts, BF16, 1.0, finish)
     xt = x.T
 

time: 191 us -> 184 us (0.963)
  waiting for transfers between devices: 51.6 us -> 39.2 us
  Pallas kernels: 93.2 us -> 98 us
    pallas_call x5 -> x10, Pallas kernels: 34.3 us -> 47.4 us  [the longest x4 23.2 us: predict(): pl.pallas_call(functools.partial(predict_body, n, held, first), out_shape...]
    ppermute x58 -> x59, waiting for transfers between devices: 51.6 us -> 39.2 us  [send(): return lax.ppermute(a, 'layer', pairs)]
    pallas_call x4 -> x3, Pallas kernels: 30 us -> 21.8 us  [backward(): pl.pallas_call(functools.partial(backward_body, n), out_shape=(half, half...]
    ppermute x58 -> x59, starting transfers between devices: 37.2 us -> 37.5 us  [send(): return lax.ppermute(a, 'layer', pairs)]
  transfers between devices with their start and end apart: 58 -> 59, of which waited for: 22 -> 20; matrix products, arithmetic and copies ran while one was open for 1% -> 1% of each run, Pallas kernels for 40% -> 46%
where the time goes in v2:
time: 184 us
  Pallas kernels  98 us (53%)
  waiting for transfers between devices  39.2 us (21%)
  starting transfers between devices  37.5 us (20%)
  local copies, waits for them, and re-layouts  3.75 us (2%)
  other arithmetic  3.43 us (2%)
    ppermute x59, waiting for transfers between devices, send(): return lax.ppermute(a, 'layer', pairs)  39.2 us
    ppermute x59, starting transfers between devices, send(): return lax.ppermute(a, 'layer', pairs)  37.5 us
    pallas_call x4, Pallas kernels, predict(): pl.pallas_call(functools.partial(predict_body, n, held, first), out_shape...  23.2 us
    pallas_call x3, Pallas kernels, backward(): pl.pallas_call(functools.partial(backward_body, n), out_shape=(half, half...  21.8 us
    pallas_call x5, Pallas kernels, gradient(): pl.pallas_call(functools.partial(gradient_body, n, scale, first), out_sha...  17.8 us
    pallas_call x3, Pallas kernels, hold(): pl.pallas_call(functools.partial(hold_body, n, kb), out_shape=(jax.ShapeD...  12.2 us
    pallas_call x5, Pallas kernels, project(): pl.pallas_call(functools.partial(project_body, first, sizes), out_shape=t...  6.67 us
    pallas_call x2, Pallas kernels, backward_held(): pl.pallas_call(functools.partial(backward_held_body, layer_count), out_sh...  6.13 us
  transfers between devices with their start and end apart: 59, of which 20 were waited for; matrix products, arithmetic and copies ran while one was open for 1% of the time, Pallas kernels for 46%

profile of v2, /device:TPU:0, one launch (start us, length us, event | category | flops | bytes accessed | tf_op | source)
XLA Modules:
  0.0 183.7 jit_solution(4769330391922033636)
XLA Ops:
  4.3 4.2 %start.1 = (bf16[512,1024]{1,0:T(8,128)(2,1)S(1)}, bf16[16,1024,256]{2,1,0:T(8,128)(2,1)S(1)}) custom-call(s32[16]{0:T(128)S(1)} %stack.147.idx_ref, bf16[512,2048]{1,0:T(8,128)(2,1)S(1)} %fusion.hot_ref, bf16[2048,1024]{1,0:T(8,128)(2,1)S(1)} %copy-done.2, bf16[1024,4096]{1,0:T(8,128)(2,1)} %basis_ref.1), custom_call_target="tpu_custom_call" | custom-call | flops 2147483648 | bytes 4194304 | tf_op jit(solution)/shard_map/start/pallas_call | solution.py:72
  11.9 3.0 %collective-permute-start.2 = (f16[256,256]{1,0:T(8,128)(2,1)S(1)}, f16[256,256]{1,0:T(8,128)(2,1)S(1)}, u32[]{:S(2)}, u32[]{:S(2)}) collective-permute-start(f16[256,256]{1,0:T(8,128)(2,1)S(1)} %get-tuple-element.113), channel_id=1, source_target_pairs={{0,4},{1,5},{4,8},{5,9},{8,12},{9,13},{12,14},{13,15},{14,10},{15,... | collective-permute-start | bytes 393224 | tf_op jit(solution)/shard_map/ppermute | solution.py:430
  21.2 4.1 %hold.4 = (bf16[8,512,1024]{2,1,0:T(8,128)(2,1)S(1)}, f32[8,128]{1,0:T(8,128)S(1)}) custom-call(s32[2]{0:T(128)S(1)} %pad_add_fusion.1.idx_ref, bf16[8,4096,1024]{2,1,0:T(8,128)(2,1)} %coeff_ref.19, f32[8,128]{1,0:T(8,128)S(1)} %slice_convert_fusion.10.mark_ref.after_ref), custom_call_target="tpu_custom_call" | custom-call | bytes 8388608 | tf_op jit(solution)/shard_map/hold/pallas_call | solution.py:225
  31.8 4.1 %hold.3 = (bf16[8,512,1024]{2,1,0:T(8,128)(2,1)S(1)}, f32[8,128]{1,0:T(8,128)S(1)}) custom-call(s32[2]{0:T(128)S(1)} %pad_add_fusion.idx_ref, bf16[8,4096,1024]{2,1,0:T(8,128)(2,1)} %coeff_ref.19, f32[8,128]{1,0:T(8,128)S(1)} %slice_convert_fusion.9.after_ref.mark_ref), custom_call_target="tpu_custom_call" | custom-call | bytes 8388608 | tf_op jit(solution)/shard_map/hold/pallas_call | solution.py:225
  40.9 6.6 %collective-permute-done.12 = f16[512,256]{1,0:T(8,128)(2,1)S(1)} collective-permute-done((f16[512,256]{1,0:T(8,128)(2,1)S(1)}, f16[512,256]{1,0:T(8,128)(2,1)S(1)}, u32[]{:S(2)}, u32[]{:S(2)}) %collective-permute-start.12) | collective-permute-done | bytes 262176 | tf_op jit(solution)/shard_map/ppermute | solution.py:430
  51.2 2.8 %predict.4 = (f32[512,1024]{1,0:T(8,128)S(1)}, f32[8,128]{1,0:T(8,128)S(1)}) custom-call(s32[1]{0:T(128)} %bitcast.14.idx_ref, bf16[8,4096,1024]{2,1,0:T(8,128)(2,1)} %coeff_ref.19, bf16[512,256]{1,0:T(8,128)(2,1)S(1)} %fusion.33.refs_0_), custom_call_target="tpu_custom_call" | custom-call | flops 1073741824 | bytes 4194304 | tf_op jit(solution)/shard_map/predict/pallas_call | solution.py:200
  54.0 4.1 %hold.5 = (bf16[8,512,1024]{2,1,0:T(8,128)(2,1)S(1)}, f32[8,128]{1,0:T(8,128)S(1)}) custom-call(s32[2]{0:T(128)S(1)} %pad_add_fusion.2.idx_ref, bf16[8,4096,1024]{2,1,0:T(8,128)(2,1)} %coeff_ref.19, f32[8,128]{1,0:T(8,128)S(1)} %get-tuple-element.65.after_ref), custom_call_target="tpu_custom_call" | custom-call | bytes 8388608 | tf_op jit(solution)/shard_map/hold/pallas_call | solution.py:225
  60.7 5.7 %predict.5 = (f32[512,1024]{1,0:T(8,128)S(1)}, f32[8,128]{1,0:T(8,128)S(1)}) custom-call(s32[3]{0:T(128)S(1)} %pad_add_fusion.3.idx_ref, bf16[8,4096,1024]{2,1,0:T(8,128)(2,1)} %coeff_ref.19, bf16[512,256]{1,0:T(8,128)(2,1)S(1)} %collective-permute-done.15.refs_0_, bf16[512,256]{1,0:T(8,128)(2,1)S(1)} %join.20.refs_1_, ...), custom_call_target="tpu_custom_call", output_to_operand_aliasing={{0}: (5, {})} | custom-call | flops 3221225472 | bytes 12582912 | tf_op jit(solution)/shard_map/predict/pallas_call | solution.py:200
  69.0 7.4 %predict.6 = (f32[512,1024]{1,0:T(8,128)S(1)}, f32[8,128]{1,0:T(8,128)S(1)}) custom-call(s32[4]{0:T(128)S(1)} %pad_add_fusion.4.idx_ref, bf16[8,4096,1024]{2,1,0:T(8,128)(2,1)} %coeff_ref.19, bf16[512,256]{1,0:T(8,128)(2,1)S(1)} %collective-permute-done.18.refs_0_, ...), custom_call_target="tpu_custom_call", output_to_operand_aliasing={{0}: (6, {})} | custom-call | flops 4294967296 | bytes 16777216 | tf_op jit(solution)/shard_map/predict/pallas_call | solution.py:200
  79.2 7.3 %predict.7 = (f32[512,1024]{1,0:T(8,128)S(1)}, f32[8,128]{1,0:T(8,128)S(1)}) custom-call(s32[2]{0:T(128)S(1)} %pad_add_fusion.5.idx_ref, bf16[8,4096,1024]{2,1,0:T(8,128)(2,1)} %coeff_ref.19, bf16[512,256]{1,0:T(8,128)(2,1)S(1)} %collective-permute-done.22.refs_0_, ...), custom_call_target="tpu_custom_call", output_to_operand_aliasing={{0}: (10, {})} | custom-call | flops 6442450944 | bytes 8388608 | tf_op jit(solution)/shard_map/predict/pallas_call | solution.py:200
  88.1 5.9 %residuals.1 = (f32[8,64,1024]{2,1,0:T(8,128)}, bf16[512,1024]{1,0:T(8,128)(2,1)S(1)}, f32[1,256,512]{2,1,0:T(8,128)S(1)}, f32[1,256,512]{2,1,0:T(8,128)S(1)}) custom-call(bf16[512,256]{1,0:T(8,128)(2,1)S(1)} %pad_maximum_fusion.2.a_ref, bf16[512,256]{1,0:T(8,128)(2,1)S(1)} %collective-permute-done.28.b_ref, ...), custom_call_target="tpu_custom_call" | custom-call | flops 4294967296 | bytes 8388608 | tf_op jit(solution)/shard_map/residuals/pallas_call | solution.py:276
  94.3 3.1 %backward_held.3 = (f32[1,256,512]{2,1,0:T(8,128)S(1)}, f32[1,256,512]{2,1,0:T(8,128)S(1)}) custom-call(bf16[512,1024]{1,0:T(8,128)(2,1)S(1)} %get-tuple-element.78.low_ref, f32[1,256,512]{2,1,0:T(8,128)S(1)} %get-tuple-element.79.mark_ref, bf16[8,512,1024]{2,1,0:T(8,128)(2,1)S(1)} %get-tuple-element.71.refs_6_.refs_0_), custom_call_target="tpu_custom_call" | custom-call | flops 2147483648 | bytes 8388608 | tf_op jit(solution)/shard_map/backward_held/pallas_call | solution.py:340
  98.5 3.1 %backward_held.2 = (f32[1,256,512]{2,1,0:T(8,128)S(1)}, f32[1,256,512]{2,1,0:T(8,128)S(1)}) custom-call(bf16[512,1024]{1,0:T(8,128)(2,1)S(1)} %get-tuple-element.78.low_ref, f32[8,128]{1,0:T(8,128)S(1)} %slice_convert_fusion.7.mark_ref, bf16[8,512,1024]{2,1,0:T(8,128)(2,1)S(1)} %get-tuple-element.72.refs_7_.refs_0_), custom_call_target="tpu_custom_call" | custom-call | flops 2147483648 | bytes 8388608 | tf_op jit(solution)/shard_map/backward_held/pallas_call | solution.py:340
  103.2 8.2 %backward.3 = (f32[2,256,512]{2,1,0:T(8,128)S(1)}, f32[2,256,512]{2,1,0:T(8,128)S(1)}) custom-call(s32[4]{0:T(128)S(1)} %pad_add_fusion.7.idx_ref, bf16[8,4096,1024]{2,1,0:T(8,128)(2,1)} %coeff_ref.19, bf16[512,1024]{1,0:T(8,128)(2,1)S(1)} %get-tuple-element.78.low_ref, f32[1,256,512]{2,1,0:T(8,128)S(1)} %get-tuple-element.81.mark_ref), custom_call_target="tpu_custom_call" | custom-call | flops 4294967296 | bytes 16777216 | tf_op jit(solution)/shard_map/backward/pallas_call | solution.py:312
  114.2 8.3 %backward.5 = (f32[2,256,512]{2,1,0:T(8,128)S(1)}, f32[2,256,512]{2,1,0:T(8,128)S(1)}) custom-call(s32[4]{0:T(128)S(1)} %pad_add_fusion.8.idx_ref, bf16[8,4096,1024]{2,1,0:T(8,128)(2,1)} %coeff_ref.19, bf16[512,1024]{1,0:T(8,128)(2,1)S(1)} %get-tuple-element.78.low_ref, f32[8,128]{1,0:T(8,128)S(1)} %slice_convert_fusion.6.mark_ref), custom_call_target="tpu_custom_call" | custom-call | flops 4294967296 | bytes 16777216 | tf_op jit(solution)/shard_map/backward/pallas_call | solution.py:312
  125.1 5.3 %backward.4 = (f32[1,256,512]{2,1,0:T(8,128)S(1)}, f32[1,256,512]{2,1,0:T(8,128)S(1)}) custom-call(s32[2]{0:T(128)S(1)} %pad_add_fusion.6.idx_ref, bf16[8,4096,1024]{2,1,0:T(8,128)(2,1)} %coeff_ref.19, bf16[512,1024]{1,0:T(8,128)(2,1)S(1)} %get-tuple-element.78.low_ref, f32[8,128]{1,0:T(8,128)S(1)} %slice_convert_fusion.5.mark_ref), custom_call_target="tpu_custom_call" | custom-call | flops 2147483648 | bytes 8388608 | tf_op jit(solution)/shard_map/backward/pallas_call | solution.py:312
  134.3 6.6 %collective-permute-done.37.right_ref = bf16[256,512]{1,0:T(8,128)(2,1)S(1)} collective-permute-done((bf16[256,512]{1,0:T(8,128)(2,1)S(1)}, bf16[256,512]{1,0:T(8,128)(2,1)S(1)}, u32[]{:S(2)}, u32[]{:S(2)}) %collective-permute-start.37) | collective-permute-done | bytes 262176 | tf_op jit(solution)/shard_map/ppermute | solution.py:430
  145.3 2.7 %gradient.5 = (f32[1024,4096]{1,0:T(8,128)}, f32[8,128]{1,0:T(8,128)S(1)}) custom-call(s32[2]{0:T(128)S(1)} %pad_add_fusion.6.idx_ref, bf16[1024,512]{1,0:T(8,128)(2,1)S(1)} %bitcast.115, bf16[512,256]{1,0:T(8,128)(2,1)S(1)} %finish.1.refs_0_, bf16[512,256]{1,0:T(8,128)(2,1)S(1)} %collective-permute-done.44.refs_1_), custom_call_target="tpu_custom_call" | custom-call | flops 536870912 | bytes 2097152 | tf_op jit(solution)/shard_map/gradient/pallas_call | solution.py:377
  148.0 3.4 %collective-permute-done.43.value_ref = bf16[512,256]{1,0:T(8,128)(2,1)S(1)} collective-permute-done((bf16[512,256]{1,0:T(8,128)(2,1)S(1)}, bf16[512,256]{1,0:T(8,128)(2,1)S(1)}, u32[]{:S(2)}, u32[]{:S(2)}) %collective-permute-start.43) | collective-permute-done | bytes 262176 | tf_op jit(solution)/shard_map/ppermute | solution.py:430
  154.7 3.9 %gradient.6 = (f32[1024,4096]{1,0:T(8,128)}, f32[8,128]{1,0:T(8,128)S(1)}) custom-call(s32[4]{0:T(128)S(1)} %pad_add_fusion.9.idx_ref, bf16[1024,512]{1,0:T(8,128)(2,1)S(1)} %bitcast.116, bf16[512,256]{1,0:T(8,128)(2,1)S(1)} %join.28.refs_0_, bf16[512,256]{1,0:T(8,128)(2,1)S(1)} %collective-permute-done.46.refs_1_, ...), custom_call_target="tpu_custom_call", output_to_operand_aliasing={{0}: (6, {})} | custom-call | flops 1073741824 | bytes 4194304 | tf_op jit(solution)/shard_map/gradient/pallas_call | solution.py:377
  164.7 3.9 %gradient.7 = (f32[1024,4096]{1,0:T(8,128)}, f32[8,128]{1,0:T(8,128)S(1)}) custom-call(s32[4]{0:T(128)S(1)} %pad_add_fusion.10.idx_ref, bf16[1024,512]{1,0:T(8,128)(2,1)S(1)} %bitcast.117, bf16[512,256]{1,0:T(8,128)(2,1)S(1)} %join.29.refs_0_, bf16[512,256]{1,0:T(8,128)(2,1)S(1)} %collective-permute-done.50.refs_1_, ...), custom_call_target="tpu_custom_call", output_to_operand_aliasing={{0}: (6, {})} | custom-call | flops 1073741824 | bytes 4194304 | tf_op jit(solution)/shard_map/gradient/pallas_call | solution.py:377
  168.6 2.7 %collective-permute-done.49.value_ref = bf16[512,256]{1,0:T(8,128)(2,1)S(1)} collective-permute-done((bf16[512,256]{1,0:T(8,128)(2,1)S(1)}, bf16[512,256]{1,0:T(8,128)(2,1)S(1)}, u32[]{:S(2)}, u32[]{:S(2)}) %collective-permute-start.49) | collective-permute-done | bytes 262176 | tf_op jit(solution)/shard_map/ppermute | solution.py:430
  174.6 3.9 %gradient.8 = (f32[1024,4096]{1,0:T(8,128)}, f32[8,128]{1,0:T(8,128)S(1)}) custom-call(s32[4]{0:T(128)S(1)} %pad_add_fusion.11.idx_ref, bf16[1024,512]{1,0:T(8,128)(2,1)S(1)} %bitcast.118, bf16[512,256]{1,0:T(8,128)(2,1)S(1)} %join.30.refs_0_, bf16[512,256]{1,0:T(8,128)(2,1)S(1)} %collective-permute-done.54.refs_1_, ...), custom_call_target="tpu_custom_call", output_to_operand_aliasing={{0}: (6, {})} | custom-call | flops 1073741824 | bytes 4194304 | tf_op jit(solution)/shard_map/gradient/pallas_call | solution.py:377
  180.3 3.3 %gradient.9 = (f32[1024,4096]{1,0:T(8,128)}, f32[8,128]{1,0:T(8,128)}) custom-call(s32[2]{0:T(128)S(1)} %copy-done.4, bf16[1024,512]{1,0:T(8,128)(2,1)S(1)} %bitcast.119, bf16[512,256]{1,0:T(8,128)(2,1)S(1)} %pad_maximum_fusion.5.refs_0_, bf16[512,256]{1,0:T(8,128)(2,1)S(1)} %collective-permute-done.58.refs_1_, ...), custom_call_target="tpu_custom_call", output_to_operand_aliasing={{0}: (4, {})} | custom-call | flops 536870912 | bytes 2097152 | tf_op jit(solution)/shard_map/gradient/pallas_call | solution.py:377
  (201 shorter events, 68.6 us)
Async XLA Ops:
  18.7 10.7 %collective-permute-start.3 = (f32[2,512,256]{2,1,0:T(8,128)S(1)}, f32[2,512,256]{2,1,0:T(8,128)S(1)}, u32[]{:S(2)}, u32[]{:S(2)}) collective-permute-start(f32[2,512,256]{2,1,0:T(8,128)S(1)} %join.17), channel_id=1, source_target_pairs={{0,1},{1,0},{2,3},{3,2},{4,5},{5,4},{6,7},{7,6},{8,9},{9,8},{10,11... | collective-permute-start | bytes 3145736 | tf_op jit(solution)/shard_map/ppermute | solution.py:430
  18.8 8.8 %collective-permute-start.4 = (f16[512,256]{1,0:T(8,128)(2,1)S(1)}, f16[512,256]{1,0:T(8,128)(2,1)S(1)}, u32[]{:S(2)}, u32[]{:S(2)}) collective-permute-start(f16[512,256]{1,0:T(8,128)(2,1)S(1)} %pad_maximum_fusion), channel_id=1, source_target_pairs={{0,4},{1,5},{4,8},{5,9},{8,12},{9,13},{12,14},{13,15},{14,10},{15,... | collective-permute-start | bytes 786440 | tf_op jit(solution)/shard_map/ppermute | solution.py:430
  29.6 8.8 %collective-permute-start.5 = (f32[2,512,256]{2,1,0:T(8,128)S(1)}, f32[2,512,256]{2,1,0:T(8,128)S(1)}, u32[]{:S(2)}, u32[]{:S(2)}) collective-permute-start(f32[2,512,256]{2,1,0:T(8,128)S(1)} %join.18), channel_id=1, source_target_pairs={{0,1},{1,0},{2,3},{3,2},{4,5},{5,4},{6,7},{7,6},{8,9},{9,8},{10,11... | collective-permute-start | bytes 3145736 | tf_op jit(solution)/shard_map/ppermute | solution.py:430
  38.7 10.2 %collective-permute-start.7 = (f32[1,512,256]{2,1,0:T(8,128)S(1)}, f32[1,512,256]{2,1,0:T(8,128)S(1)}, u32[]{:S(2)}, u32[]{:S(2)}) collective-permute-start(f32[1,512,256]{2,1,0:T(8,128)S(1)} %join.19), channel_id=1, source_target_pairs={{0,1},{1,0},{2,3},{3,2},{4,5},{5,4},{6,7},{7,6},{8,9},{9,8},{10,11... | collective-permute-start | bytes 1572872 | tf_op jit(solution)/shard_map/ppermute | solution.py:430
  49.0 9.1 %collective-permute-start.13 = (bf16[512,256]{1,0:T(8,128)(2,1)S(1)}, bf16[512,256]{1,0:T(8,128)(2,1)S(1)}, u32[]{:S(2)}, u32[]{:S(2)}) collective-permute-start(bf16[512,256]{1,0:T(8,128)(2,1)S(1)} %fusion.33.refs_0_), channel_id=1, source_target_pairs={{0,4},{1,5},{4,8},{5,9},{8,12},{9,13},{12,14},{13,15},{14,10},{15,... | collective-permute-start | bytes 786440 | tf_op jit(solution)/shard_map/ppermute | solution.py:430
  49.4 11.4 %collective-permute-start.15 = (bf16[512,256]{1,0:T(8,128)(2,1)S(1)}, bf16[512,256]{1,0:T(8,128)(2,1)S(1)}, u32[]{:S(2)}, u32[]{:S(2)}) collective-permute-start(bf16[512,256]{1,0:T(8,128)(2,1)S(1)} %fusion.33.refs_0_), channel_id=1, source_target_pairs={{0,1},{1,0},{2,3},{3,2},{4,5},{5,4},{6,7},{7,6},{8,9},{9,8},{10,11... | collective-permute-start | bytes 786440 | tf_op jit(solution)/shard_map/ppermute | solution.py:430
  49.4 9.2 %collective-permute-start.16 = (bf16[512,256]{1,0:T(8,128)(2,1)S(1)}, bf16[512,256]{1,0:T(8,128)(2,1)S(1)}, u32[]{:S(2)}, u32[]{:S(2)}) collective-permute-start(bf16[512,256]{1,0:T(8,128)(2,1)S(1)} %fusion.33.refs_0_), channel_id=1, source_target_pairs={{0,2},{1,3},{4,0},{5,1},{8,4},{9,5},{12,8},{13,9},{14,12},{15,13},... | collective-permute-start | bytes 786440 | tf_op jit(solution)/shard_map/ppermute | solution.py:430
  58.5 10.4 %collective-permute-start.18 = (bf16[512,256]{1,0:T(8,128)(2,1)S(1)}, bf16[512,256]{1,0:T(8,128)(2,1)S(1)}, u32[]{:S(2)}, u32[]{:S(2)}) collective-permute-start(bf16[512,256]{1,0:T(8,128)(2,1)S(1)} %join.20.refs_1_), channel_id=1, source_target_pairs={{0,1},{1,0},{2,3},{3,2},{4,5},{5,4},{6,7},{7,6},{8,9},{9,8},{10,11... | collective-permute-start | bytes 786440 | tf_op jit(solution)/shard_map/ppermute | solution.py:430
  58.5 10.4 %collective-permute-start.19 = (bf16[512,256]{1,0:T(8,128)(2,1)S(1)}, bf16[512,256]{1,0:T(8,128)(2,1)S(1)}, u32[]{:S(2)}, u32[]{:S(2)}) collective-permute-start(bf16[512,256]{1,0:T(8,128)(2,1)S(1)} %collective-permute-done.16.refs_2_), channel_id=1, source_target_pairs={{0,1},{1,0},{2,3},{3,2},{4,5},{5,4},{6,7},{7,6},{8,9},{9,8},{10,11... | collective-permute-start | bytes 786440 | tf_op jit(solution)/shard_map/ppermute | solution.py:430
  66.6 9.7 %collective-permute-start.17 = (bf16[512,256]{1,0:T(8,128)(2,1)S(1)}, bf16[512,256]{1,0:T(8,128)(2,1)S(1)}, u32[]{:S(2)}, u32[]{:S(2)}) collective-permute-start(bf16[512,256]{1,0:T(8,128)(2,1)S(1)} %join.21.refs_2_), channel_id=1, source_target_pairs={{0,4},{1,5},{4,8},{5,9},{8,12},{9,13},{12,14},{13,15},{14,10},{15,... | collective-permute-start | bytes 786440 | tf_op jit(solution)/shard_map/ppermute | solution.py:430
  67.0 10.6 %collective-permute-start.22 = (bf16[512,256]{1,0:T(8,128)(2,1)S(1)}, bf16[512,256]{1,0:T(8,128)(2,1)S(1)}, u32[]{:S(2)}, u32[]{:S(2)}) collective-permute-start(bf16[512,256]{1,0:T(8,128)(2,1)S(1)} %join.21.refs_2_), channel_id=1, source_target_pairs={{0,1},{1,0},{2,3},{3,2},{4,5},{5,4},{6,7},{7,6},{8,9},{9,8},{10,11... | collective-permute-start | bytes 786440 | tf_op jit(solution)/shard_map/ppermute | solution.py:430
  67.3 9.6 %collective-permute-start.24 = (bf16[512,256]{1,0:T(8,128)(2,1)S(1)}, bf16[512,256]{1,0:T(8,128)(2,1)S(1)}, u32[]{:S(2)}, u32[]{:S(2)}) collective-permute-start(bf16[512,256]{1,0:T(8,128)(2,1)S(1)} %collective-permute-done.20.refs_3_), channel_id=1, source_target_pairs={{0,2},{1,3},{4,0},{5,1},{8,4},{9,5},{12,8},{13,9},{14,12},{15,13},... | collective-permute-start | bytes 786440 | tf_op jit(solution)/shard_map/ppermute | solution.py:430
  69.0 10.2 %collective-permute-start.23 = (bf16[512,256]{1,0:T(8,128)(2,1)S(1)}, bf16[512,256]{1,0:T(8,128)(2,1)S(1)}, u32[]{:S(2)}, u32[]{:S(2)}) collective-permute-start(bf16[512,256]{1,0:T(8,128)(2,1)S(1)} %collective-permute-done.20.refs_3_), channel_id=1, source_target_pairs={{0,1},{1,0},{2,3},{3,2},{4,5},{5,4},{6,7},{7,6},{8,9},{9,8},{10,11... | collective-permute-start | bytes 786440 | tf_op jit(solution)/shard_map/ppermute | solution.py:430
  77.0 9.4 %collective-permute-start.21 = (bf16[256,256]{1,0:T(8,128)(2,1)S(1)}, bf16[256,256]{1,0:T(8,128)(2,1)S(1)}, u32[]{:S(2)}, u32[]{:S(2)}) collective-permute-start(bf16[256,256]{1,0:T(8,128)(2,1)S(1)} %slice.246), channel_id=1, source_target_pairs={{0,4},{1,5},{4,8},{5,9},{8,12},{9,13},{12,14},{13,15},{14,10},{15,... | collective-permute-start | bytes 393224 | tf_op jit(solution)/shard_map/ppermute | solution.py:430
  77.6 8.9 %collective-permute-start.27 = (bf16[256,256]{1,0:T(8,128)(2,1)S(1)}, bf16[256,256]{1,0:T(8,128)(2,1)S(1)}, u32[]{:S(2)}, u32[]{:S(2)}) collective-permute-start(bf16[256,256]{1,0:T(8,128)(2,1)S(1)} %slice.247), channel_id=1, source_target_pairs={{0,2},{1,3},{4,0},{5,1},{8,4},{9,5},{12,8},{13,9},{14,12},{15,13},... | collective-permute-start | bytes 393224 | tf_op jit(solution)/shard_map/ppermute | solution.py:430
  97.5 13.9 %collective-permute-start.30 = (f32[1,256,512]{2,1,0:T(8,128)S(1)}, f32[1,256,512]{2,1,0:T(8,128)S(1)}, u32[]{:S(2)}, u32[]{:S(2)}) collective-permute-start(f32[1,256,512]{2,1,0:T(8,128)S(1)} %join.24), channel_id=1, source_target_pairs={{0,1},{1,0},{2,3},{3,2},{4,5},{5,4},{6,7},{7,6},{8,9},{9,8},{10,11... | collective-permute-start | bytes 1572872 | tf_op jit(solution)/shard_map/ppermute | solution.py:430
  98.0 13.6 %collective-permute-start.31 = (bf16[128,512]{1,0:T(8,128)(2,1)S(1)}, bf16[128,512]{1,0:T(8,128)(2,1)S(1)}, u32[]{:S(2)}, u32[]{:S(2)}) collective-permute-start(bf16[128,512]{1,0:T(8,128)(2,1)S(1)} %get-tuple-element.111), channel_id=1, source_target_pairs={{0,4},{1,5},{4,8},{5,9},{8,12},{9,13},{12,14},{13,15},{14,10},{15,... | collective-permute-start | bytes 393224 | tf_op jit(solution)/shard_map/ppermute | solution.py:430
  101.5 10.9 %collective-permute-start.38 = (f32[1,256,512]{2,1,0:T(8,128)S(1)}, f32[1,256,512]{2,1,0:T(8,128)S(1)}, u32[]{:S(2)}, u32[]{:S(2)}) collective-permute-start(f32[1,256,512]{2,1,0:T(8,128)S(1)} %get-tuple-element.90), channel_id=1, source_target_pairs={{0,1},{1,0},{2,3},{3,2},{4,5},{5,4},{6,7},{7,6},{8,9},{9,8},{10,11... | collective-permute-start | bytes 1572872 | tf_op jit(solution)/shard_map/ppermute | solution.py:430
  101.6 10.9 %collective-permute-start.39 = (bf16[128,512]{1,0:T(8,128)(2,1)S(1)}, bf16[128,512]{1,0:T(8,128)(2,1)S(1)}, u32[]{:S(2)}, u32[]{:S(2)}) collective-permute-start(bf16[128,512]{1,0:T(8,128)(2,1)S(1)} %get-tuple-element.110), channel_id=1, source_target_pairs={{0,2},{1,3},{4,0},{5,1},{8,4},{9,5},{12,8},{13,9},{14,12},{15,13},... | collective-permute-start | bytes 393224 | tf_op jit(solution)/shard_map/ppermute | solution.py:430
  111.6 10.9 %collective-permute-start.32 = (f32[2,256,512]{2,1,0:T(8,128)S(1)}, f32[2,256,512]{2,1,0:T(8,128)S(1)}, u32[]{:S(2)}, u32[]{:S(2)}) collective-permute-start(f32[2,256,512]{2,1,0:T(8,128)S(1)} %join.25), channel_id=1, source_target_pairs={{0,1},{1,0},{2,3},{3,2},{4,5},{5,4},{6,7},{7,6},{8,9},{9,8},{10,11... | collective-permute-start | bytes 3145736 | tf_op jit(solution)/shard_map/ppermute | solution.py:430
  111.9 10.6 %collective-permute-start.33 = (bf16[256,512]{1,0:T(8,128)(2,1)S(1)}, bf16[256,512]{1,0:T(8,128)(2,1)S(1)}, u32[]{:S(2)}, u32[]{:S(2)}) collective-permute-start(bf16[256,512]{1,0:T(8,128)(2,1)S(1)} %pad_maximum_fusion.3), channel_id=1, source_target_pairs={{0,4},{1,5},{4,8},{5,9},{8,12},{9,13},{12,14},{13,15},{14,10},{15,... | collective-permute-start | bytes 786440 | tf_op jit(solution)/shard_map/ppermute | solution.py:430
  112.6 9.9 %collective-permute-start.40 = (bf16[256,512]{1,0:T(8,128)(2,1)S(1)}, bf16[256,512]{1,0:T(8,128)(2,1)S(1)}, u32[]{:S(2)}, u32[]{:S(2)}) collective-permute-start(bf16[256,512]{1,0:T(8,128)(2,1)S(1)} %pad_maximum_fusion.4), channel_id=1, source_target_pairs={{0,2},{1,3},{4,0},{5,1},{8,4},{9,5},{12,8},{13,9},{14,12},{15,13},... | collective-permute-start | bytes 786440 | tf_op jit(solution)/shard_map/ppermute | solution.py:430
  122.8 9.0 %collective-permute-start.34 = (f32[2,256,512]{2,1,0:T(8,128)S(1)}, f32[2,256,512]{2,1,0:T(8,128)S(1)}, u32[]{:S(2)}, u32[]{:S(2)}) collective-permute-start(f32[2,256,512]{2,1,0:T(8,128)S(1)} %join.26), channel_id=1, source_target_pairs={{0,1},{1,0},{2,3},{3,2},{4,5},{5,4},{6,7},{7,6},{8,9},{9,8},{10,11... | collective-permute-start | bytes 3145736 | tf_op jit(solution)/shard_map/ppermute | solution.py:430
  132.2 10.2 %collective-permute-start.36 = (f32[1,256,512]{2,1,0:T(8,128)S(1)}, f32[1,256,512]{2,1,0:T(8,128)S(1)}, u32[]{:S(2)}, u32[]{:S(2)}) collective-permute-start(f32[1,256,512]{2,1,0:T(8,128)S(1)} %join.27), channel_id=1, source_target_pairs={{0,1},{1,0},{2,3},{3,2},{4,5},{5,4},{6,7},{7,6},{8,9},{9,8},{10,11... | collective-permute-start | bytes 1572872 | tf_op jit(solution)/shard_map/ppermute | solution.py:430
  (41 other events, 275.2 us)

commit v3 on v2

--- a/solution.py
+++ b/solution.py
@@ -259,14 +259,16 @@
 
     @pl.loop(0, layer_count, step=2)
     def _(l):
-        for j in range(2):
-            span = rows_of(l + j, toks)
-            part = predicted(l + j, span, (a_ref, b_ref), 0, None, 1, (tiles_ref,))
+        spans = [rows_of(l + j, toks) for j in range(2)]
+        parts = [predicted(l + j, spans[j], (a_ref, b_ref), 0, None, 1, (tiles_ref,)) for j in range(2)]
+        lows = []
+        for j, (span, part) in enumerate(zip(spans, parts)):
             res = target_ref[l + j].astype(F32) - (acc_ref[span, :] + part)
             res_ref[l + j] = res
-            low_ref[span, :] = res.astype(BF16)
-        pair = pl.ds(pl.multiple_of(l * toks, 2 * toks), 2 * toks)
-        back_blocks(low_ref[pair, :], tiles_ref, l, [keep_ref.at[0], send_ref.at[0]], toks)
+            lows.append(res.astype(BF16))
+            low_ref[span, :] = lows[j]
+        low = jnp.concatenate(lows, axis=0)
+        back_blocks(low, tiles_ref, l, [keep_ref.at[0], send_ref.at[0]], toks)
 
 
 def residuals(pieces, tiles, targets, acc):
@@ -325,11 +327,13 @@
     tiles, (keep_ref, send_ref) = refs[:-2], refs[-2:]
     toks = low_ref.shape[0] // layer_count
 
-    @pl.loop(0, layer_count, step=2)
-    def _(l):
-        pair = pl.ds(pl.multiple_of(l * toks, 2 * toks), 2 * toks)
-        for i, tile in enumerate(tiles):
-            back_blocks(low_ref[pair, :], tile, l, [keep_ref.at[i], send_ref.at[i]], toks)
+    @pl.loop(0, layer_count, step=4)
+    def _(first):
+        for j in range(0, 4, 2):
+            l = first + j
+            pair = pl.ds(pl.multiple_of(l * toks, 2 * toks), 2 * toks)
+            for i, tile in enumerate(tiles):
+                back_blocks(low_ref[pair, :], tile, l, [keep_ref.at[i], send_ref.at[i]], toks)
 
 
 def backward_held(tiles, low, mark, kb):

time: 184 us -> 183 us (level)
  transfers between devices with their start and end apart: 59 -> 59, of which waited for: 20 -> 20; matrix products, arithmetic and copies ran while one was open for 1% -> 1% of each run, Pallas kernels for 46% -> 45%
where the time goes in v3:
time: 183 us; the launch traced here: 182 us
  Pallas kernels  96.6 us (53%)
  waiting for transfers between devices  39.2 us (21%)
  starting transfers between devices  37.5 us (20%)
  local copies, waits for them, and re-layouts  3.75 us (2%)
  other arithmetic  3.43 us (2%)
    ppermute x59, waiting for transfers between devices, send(): return lax.ppermute(a, 'layer', pairs)  39.2 us
    ppermute x59, starting transfers between devices, send(): return lax.ppermute(a, 'layer', pairs)  37.5 us
    pallas_call x4, Pallas kernels, predict(): pl.pallas_call(functools.partial(predict_body, n, held, first), out_shape...  23.2 us
    pallas_call x3, Pallas kernels, backward(): pl.pallas_call(functools.partial(backward_body, n), out_shape=(half, half...  21.8 us
    pallas_call x5, Pallas kernels, gradient(): pl.pallas_call(functools.partial(gradient_body, n, scale, first), out_sha...  17.8 us
    pallas_call x3, Pallas kernels, hold(): pl.pallas_call(functools.partial(hold_body, n, kb), out_shape=(jax.ShapeD...  12.2 us
    pallas_call x5, Pallas kernels, project(): pl.pallas_call(functools.partial(project_body, first, sizes), out_shape=t...  6.67 us
    pallas_call x1, Pallas kernels, residuals(): pl.pallas_call(residual_body, out_shape=(jax.ShapeDtypeStruct(targets.sha...  5.35 us
  transfers between devices with their start and end apart: 59, of which 20 were waited for; matrix products, arithmetic and copies ran while one was open for 1% of the time, Pallas kernels for 45%

profile of v3, /device:TPU:0, one launch (start us, length us, event | category | flops | bytes accessed | tf_op | source)
XLA Modules:
  0.0 182.3 jit_solution(11690973168106550614)
XLA Ops:
  4.3 4.2 %start.1 = (bf16[512,1024]{1,0:T(8,128)(2,1)S(1)}, bf16[16,1024,256]{2,1,0:T(8,128)(2,1)S(1)}) custom-call(s32[16]{0:T(128)S(1)} %stack.147.idx_ref, bf16[512,2048]{1,0:T(8,128)(2,1)S(1)} %fusion.hot_ref, bf16[2048,1024]{1,0:T(8,128)(2,1)S(1)} %copy-done.2, bf16[1024,4096]{1,0:T(8,128)(2,1)} %basis_ref.1), custom_call_target="tpu_custom_call" | custom-call | flops 2147483648 | bytes 4194304 | tf_op jit(solution)/shard_map/start/pallas_call | solution.py:72
  11.9 3.0 %collective-permute-start.2 = (f16[256,256]{1,0:T(8,128)(2,1)S(1)}, f16[256,256]{1,0:T(8,128)(2,1)S(1)}, u32[]{:S(2)}, u32[]{:S(2)}) collective-permute-start(f16[256,256]{1,0:T(8,128)(2,1)S(1)} %get-tuple-element.113), channel_id=1, source_target_pairs={{0,4},{1,5},{4,8},{5,9},{8,12},{9,13},{12,14},{13,15},{14,10},{15,... | collective-permute-start | bytes 393224 | tf_op jit(solution)/shard_map/ppermute | solution.py:434
  21.2 4.1 %hold.4 = (bf16[8,512,1024]{2,1,0:T(8,128)(2,1)S(1)}, f32[8,128]{1,0:T(8,128)S(1)}) custom-call(s32[2]{0:T(128)S(1)} %pad_add_fusion.1.idx_ref, bf16[8,4096,1024]{2,1,0:T(8,128)(2,1)} %coeff_ref.19, f32[8,128]{1,0:T(8,128)S(1)} %slice_convert_fusion.10.mark_ref.after_ref), custom_call_target="tpu_custom_call" | custom-call | bytes 8388608 | tf_op jit(solution)/shard_map/hold/pallas_call | solution.py:225
  31.8 4.1 %hold.3 = (bf16[8,512,1024]{2,1,0:T(8,128)(2,1)S(1)}, f32[8,128]{1,0:T(8,128)S(1)}) custom-call(s32[2]{0:T(128)S(1)} %pad_add_fusion.idx_ref, bf16[8,4096,1024]{2,1,0:T(8,128)(2,1)} %coeff_ref.19, f32[8,128]{1,0:T(8,128)S(1)} %slice_convert_fusion.9.after_ref.mark_ref), custom_call_target="tpu_custom_call" | custom-call | bytes 8388608 | tf_op jit(solution)/shard_map/hold/pallas_call | solution.py:225
  40.9 6.6 %collective-permute-done.12 = f16[512,256]{1,0:T(8,128)(2,1)S(1)} collective-permute-done((f16[512,256]{1,0:T(8,128)(2,1)S(1)}, f16[512,256]{1,0:T(8,128)(2,1)S(1)}, u32[]{:S(2)}, u32[]{:S(2)}) %collective-permute-start.12) | collective-permute-done | bytes 262176 | tf_op jit(solution)/shard_map/ppermute | solution.py:434
  51.2 2.8 %predict.4 = (f32[512,1024]{1,0:T(8,128)S(1)}, f32[8,128]{1,0:T(8,128)S(1)}) custom-call(s32[1]{0:T(128)} %bitcast.14.idx_ref, bf16[8,4096,1024]{2,1,0:T(8,128)(2,1)} %coeff_ref.19, bf16[512,256]{1,0:T(8,128)(2,1)S(1)} %fusion.33.refs_0_), custom_call_target="tpu_custom_call" | custom-call | flops 1073741824 | bytes 4194304 | tf_op jit(solution)/shard_map/predict/pallas_call | solution.py:200
  54.0 4.1 %hold.5 = (bf16[8,512,1024]{2,1,0:T(8,128)(2,1)S(1)}, f32[8,128]{1,0:T(8,128)S(1)}) custom-call(s32[2]{0:T(128)S(1)} %pad_add_fusion.2.idx_ref, bf16[8,4096,1024]{2,1,0:T(8,128)(2,1)} %coeff_ref.19, f32[8,128]{1,0:T(8,128)S(1)} %get-tuple-element.65.after_ref), custom_call_target="tpu_custom_call" | custom-call | bytes 8388608 | tf_op jit(solution)/shard_map/hold/pallas_call | solution.py:225
  60.7 5.7 %predict.5 = (f32[512,1024]{1,0:T(8,128)S(1)}, f32[8,128]{1,0:T(8,128)S(1)}) custom-call(s32[3]{0:T(128)S(1)} %pad_add_fusion.3.idx_ref, bf16[8,4096,1024]{2,1,0:T(8,128)(2,1)} %coeff_ref.19, bf16[512,256]{1,0:T(8,128)(2,1)S(1)} %collective-permute-done.15.refs_0_, bf16[512,256]{1,0:T(8,128)(2,1)S(1)} %join.20.refs_1_, ...), custom_call_target="tpu_custom_call", output_to_operand_aliasing={{0}: (5, {})} | custom-call | flops 3221225472 | bytes 12582912 | tf_op jit(solution)/shard_map/predict/pallas_call | solution.py:200
  69.0 7.4 %predict.6 = (f32[512,1024]{1,0:T(8,128)S(1)}, f32[8,128]{1,0:T(8,128)S(1)}) custom-call(s32[4]{0:T(128)S(1)} %pad_add_fusion.4.idx_ref, bf16[8,4096,1024]{2,1,0:T(8,128)(2,1)} %coeff_ref.19, bf16[512,256]{1,0:T(8,128)(2,1)S(1)} %collective-permute-done.18.refs_0_, ...), custom_call_target="tpu_custom_call", output_to_operand_aliasing={{0}: (6, {})} | custom-call | flops 4294967296 | bytes 16777216 | tf_op jit(solution)/shard_map/predict/pallas_call | solution.py:200
  79.2 7.3 %predict.7 = (f32[512,1024]{1,0:T(8,128)S(1)}, f32[8,128]{1,0:T(8,128)S(1)}) custom-call(s32[2]{0:T(128)S(1)} %pad_add_fusion.5.idx_ref, bf16[8,4096,1024]{2,1,0:T(8,128)(2,1)} %coeff_ref.19, bf16[512,256]{1,0:T(8,128)(2,1)S(1)} %collective-permute-done.22.refs_0_, ...), custom_call_target="tpu_custom_call", output_to_operand_aliasing={{0}: (10, {})} | custom-call | flops 6442450944 | bytes 8388608 | tf_op jit(solution)/shard_map/predict/pallas_call | solution.py:200
  88.1 5.4 %residuals.1 = (f32[8,64,1024]{2,1,0:T(8,128)}, bf16[512,1024]{1,0:T(8,128)(2,1)S(1)}, f32[1,256,512]{2,1,0:T(8,128)S(1)}, f32[1,256,512]{2,1,0:T(8,128)S(1)}) custom-call(bf16[512,256]{1,0:T(8,128)(2,1)S(1)} %pad_maximum_fusion.2.a_ref, bf16[512,256]{1,0:T(8,128)(2,1)S(1)} %collective-permute-done.28.b_ref, ...), custom_call_target="tpu_custom_call" | custom-call | flops 4294967296 | bytes 8388608 | tf_op jit(solution)/shard_map/residuals/pallas_call | solution.py:278
  93.8 2.6 %backward_held.3 = (f32[1,256,512]{2,1,0:T(8,128)S(1)}, f32[1,256,512]{2,1,0:T(8,128)S(1)}) custom-call(bf16[512,1024]{1,0:T(8,128)(2,1)S(1)} %get-tuple-element.78.low_ref, f32[1,256,512]{2,1,0:T(8,128)S(1)} %get-tuple-element.79.mark_ref, bf16[8,512,1024]{2,1,0:T(8,128)(2,1)S(1)} %get-tuple-element.71.refs_6_.refs_0_), custom_call_target="tpu_custom_call" | custom-call | flops 2147483648 | bytes 8388608 | tf_op jit(solution)/shard_map/backward_held/pallas_call | solution.py:344
  101.8 8.2 %backward.3 = (f32[2,256,512]{2,1,0:T(8,128)S(1)}, f32[2,256,512]{2,1,0:T(8,128)S(1)}) custom-call(s32[4]{0:T(128)S(1)} %pad_add_fusion.7.idx_ref, bf16[8,4096,1024]{2,1,0:T(8,128)(2,1)} %coeff_ref.19, bf16[512,1024]{1,0:T(8,128)(2,1)S(1)} %get-tuple-element.78.low_ref, f32[1,256,512]{2,1,0:T(8,128)S(1)} %get-tuple-element.81.mark_ref), custom_call_target="tpu_custom_call" | custom-call | flops 4294967296 | bytes 16777216 | tf_op jit(solution)/shard_map/backward/pallas_call | solution.py:314
  112.8 8.2 %backward.5 = (f32[2,256,512]{2,1,0:T(8,128)S(1)}, f32[2,256,512]{2,1,0:T(8,128)S(1)}) custom-call(s32[4]{0:T(128)S(1)} %pad_add_fusion.8.idx_ref, bf16[8,4096,1024]{2,1,0:T(8,128)(2,1)} %coeff_ref.19, bf16[512,1024]{1,0:T(8,128)(2,1)S(1)} %get-tuple-element.78.low_ref, f32[8,128]{1,0:T(8,128)S(1)} %slice_convert_fusion.6.mark_ref), custom_call_target="tpu_custom_call" | custom-call | flops 4294967296 | bytes 16777216 | tf_op jit(solution)/shard_map/backward/pallas_call | solution.py:314
  123.7 5.3 %backward.4 = (f32[1,256,512]{2,1,0:T(8,128)S(1)}, f32[1,256,512]{2,1,0:T(8,128)S(1)}) custom-call(s32[2]{0:T(128)S(1)} %pad_add_fusion.6.idx_ref, bf16[8,4096,1024]{2,1,0:T(8,128)(2,1)} %coeff_ref.19, bf16[512,1024]{1,0:T(8,128)(2,1)S(1)} %get-tuple-element.78.low_ref, f32[8,128]{1,0:T(8,128)S(1)} %slice_convert_fusion.5.mark_ref), custom_call_target="tpu_custom_call" | custom-call | flops 2147483648 | bytes 8388608 | tf_op jit(solution)/shard_map/backward/pallas_call | solution.py:314
  132.9 6.6 %collective-permute-done.37.right_ref = bf16[256,512]{1,0:T(8,128)(2,1)S(1)} collective-permute-done((bf16[256,512]{1,0:T(8,128)(2,1)S(1)}, bf16[256,512]{1,0:T(8,128)(2,1)S(1)}, u32[]{:S(2)}, u32[]{:S(2)}) %collective-permute-start.37) | collective-permute-done | bytes 262176 | tf_op jit(solution)/shard_map/ppermute | solution.py:434
  143.9 2.7 %gradient.5 = (f32[1024,4096]{1,0:T(8,128)}, f32[8,128]{1,0:T(8,128)S(1)}) custom-call(s32[2]{0:T(128)S(1)} %pad_add_fusion.6.idx_ref, bf16[1024,512]{1,0:T(8,128)(2,1)S(1)} %bitcast.115, bf16[512,256]{1,0:T(8,128)(2,1)S(1)} %finish.1.refs_0_, bf16[512,256]{1,0:T(8,128)(2,1)S(1)} %collective-permute-done.44.refs_1_), custom_call_target="tpu_custom_call" | custom-call | flops 536870912 | bytes 2097152 | tf_op jit(solution)/shard_map/gradient/pallas_call | solution.py:381
  146.6 3.4 %collective-permute-done.43.value_ref = bf16[512,256]{1,0:T(8,128)(2,1)S(1)} collective-permute-done((bf16[512,256]{1,0:T(8,128)(2,1)S(1)}, bf16[512,256]{1,0:T(8,128)(2,1)S(1)}, u32[]{:S(2)}, u32[]{:S(2)}) %collective-permute-start.43) | collective-permute-done | bytes 262176 | tf_op jit(solution)/shard_map/ppermute | solution.py:434
  153.3 3.9 %gradient.6 = (f32[1024,4096]{1,0:T(8,128)}, f32[8,128]{1,0:T(8,128)S(1)}) custom-call(s32[4]{0:T(128)S(1)} %pad_add_fusion.9.idx_ref, bf16[1024,512]{1,0:T(8,128)(2,1)S(1)} %bitcast.116, bf16[512,256]{1,0:T(8,128)(2,1)S(1)} %join.28.refs_0_, bf16[512,256]{1,0:T(8,128)(2,1)S(1)} %collective-permute-done.46.refs_1_, ...), custom_call_target="tpu_custom_call", output_to_operand_aliasing={{0}: (6, {})} | custom-call | flops 1073741824 | bytes 4194304 | tf_op jit(solution)/shard_map/gradient/pallas_call | solution.py:381
  157.2 2.7 %collective-permute-done.45.value_ref = bf16[512,256]{1,0:T(8,128)(2,1)S(1)} collective-permute-done((bf16[512,256]{1,0:T(8,128)(2,1)S(1)}, bf16[512,256]{1,0:T(8,128)(2,1)S(1)}, u32[]{:S(2)}, u32[]{:S(2)}) %collective-permute-start.45) | collective-permute-done | bytes 262176 | tf_op jit(solution)/shard_map/ppermute | solution.py:434
  163.3 3.9 %gradient.7 = (f32[1024,4096]{1,0:T(8,128)}, f32[8,128]{1,0:T(8,128)S(1)}) custom-call(s32[4]{0:T(128)S(1)} %pad_add_fusion.10.idx_ref, bf16[1024,512]{1,0:T(8,128)(2,1)S(1)} %bitcast.117, bf16[512,256]{1,0:T(8,128)(2,1)S(1)} %join.29.refs_0_, bf16[512,256]{1,0:T(8,128)(2,1)S(1)} %collective-permute-done.50.refs_1_, ...), custom_call_target="tpu_custom_call", output_to_operand_aliasing={{0}: (6, {})} | custom-call | flops 1073741824 | bytes 4194304 | tf_op jit(solution)/shard_map/gradient/pallas_call | solution.py:381
  167.2 2.7 %collective-permute-done.49.value_ref = bf16[512,256]{1,0:T(8,128)(2,1)S(1)} collective-permute-done((bf16[512,256]{1,0:T(8,128)(2,1)S(1)}, bf16[512,256]{1,0:T(8,128)(2,1)S(1)}, u32[]{:S(2)}, u32[]{:S(2)}) %collective-permute-start.49) | collective-permute-done | bytes 262176 | tf_op jit(solution)/shard_map/ppermute | solution.py:434
  173.2 3.9 %gradient.8 = (f32[1024,4096]{1,0:T(8,128)}, f32[8,128]{1,0:T(8,128)S(1)}) custom-call(s32[4]{0:T(128)S(1)} %pad_add_fusion.11.idx_ref, bf16[1024,512]{1,0:T(8,128)(2,1)S(1)} %bitcast.118, bf16[512,256]{1,0:T(8,128)(2,1)S(1)} %join.30.refs_0_, bf16[512,256]{1,0:T(8,128)(2,1)S(1)} %collective-permute-done.54.refs_1_, ...), custom_call_target="tpu_custom_call", output_to_operand_aliasing={{0}: (6, {})} | custom-call | flops 1073741824 | bytes 4194304 | tf_op jit(solution)/shard_map/gradient/pallas_call | solution.py:381
  178.9 3.3 %gradient.9 = (f32[1024,4096]{1,0:T(8,128)}, f32[8,128]{1,0:T(8,128)}) custom-call(s32[2]{0:T(128)S(1)} %copy-done.4, bf16[1024,512]{1,0:T(8,128)(2,1)S(1)} %bitcast.119, bf16[512,256]{1,0:T(8,128)(2,1)S(1)} %pad_maximum_fusion.5.refs_0_, bf16[512,256]{1,0:T(8,128)(2,1)S(1)} %collective-permute-done.58.refs_1_, ...), custom_call_target="tpu_custom_call", output_to_operand_aliasing={{0}: (4, {})} | custom-call | flops 536870912 | bytes 2097152 | tf_op jit(solution)/shard_map/gradient/pallas_call | solution.py:381
  (201 shorter events, 68.6 us)
Async XLA Ops:
  18.7 10.7 %collective-permute-start.3 = (f32[2,512,256]{2,1,0:T(8,128)S(1)}, f32[2,512,256]{2,1,0:T(8,128)S(1)}, u32[]{:S(2)}, u32[]{:S(2)}) collective-permute-start(f32[2,512,256]{2,1,0:T(8,128)S(1)} %join.17), channel_id=1, source_target_pairs={{0,1},{1,0},{2,3},{3,2},{4,5},{5,4},{6,7},{7,6},{8,9},{9,8},{10,11... | collective-permute-start | bytes 3145736 | tf_op jit(solution)/shard_map/ppermute | solution.py:434
  18.8 8.8 %collective-permute-start.4 = (f16[512,256]{1,0:T(8,128)(2,1)S(1)}, f16[512,256]{1,0:T(8,128)(2,1)S(1)}, u32[]{:S(2)}, u32[]{:S(2)}) collective-permute-start(f16[512,256]{1,0:T(8,128)(2,1)S(1)} %pad_maximum_fusion), channel_id=1, source_target_pairs={{0,4},{1,5},{4,8},{5,9},{8,12},{9,13},{12,14},{13,15},{14,10},{15,... | collective-permute-start | bytes 786440 | tf_op jit(solution)/shard_map/ppermute | solution.py:434
  29.6 8.8 %collective-permute-start.5 = (f32[2,512,256]{2,1,0:T(8,128)S(1)}, f32[2,512,256]{2,1,0:T(8,128)S(1)}, u32[]{:S(2)}, u32[]{:S(2)}) collective-permute-start(f32[2,512,256]{2,1,0:T(8,128)S(1)} %join.18), channel_id=1, source_target_pairs={{0,1},{1,0},{2,3},{3,2},{4,5},{5,4},{6,7},{7,6},{8,9},{9,8},{10,11... | collective-permute-start | bytes 3145736 | tf_op jit(solution)/shard_map/ppermute | solution.py:434
  38.7 10.2 %collective-permute-start.7 = (f32[1,512,256]{2,1,0:T(8,128)S(1)}, f32[1,512,256]{2,1,0:T(8,128)S(1)}, u32[]{:S(2)}, u32[]{:S(2)}) collective-permute-start(f32[1,512,256]{2,1,0:T(8,128)S(1)} %join.19), channel_id=1, source_target_pairs={{0,1},{1,0},{2,3},{3,2},{4,5},{5,4},{6,7},{7,6},{8,9},{9,8},{10,11... | collective-permute-start | bytes 1572872 | tf_op jit(solution)/shard_map/ppermute | solution.py:434
  49.0 9.1 %collective-permute-start.13 = (bf16[512,256]{1,0:T(8,128)(2,1)S(1)}, bf16[512,256]{1,0:T(8,128)(2,1)S(1)}, u32[]{:S(2)}, u32[]{:S(2)}) collective-permute-start(bf16[512,256]{1,0:T(8,128)(2,1)S(1)} %fusion.33.refs_0_), channel_id=1, source_target_pairs={{0,4},{1,5},{4,8},{5,9},{8,12},{9,13},{12,14},{13,15},{14,10},{15,... | collective-permute-start | bytes 786440 | tf_op jit(solution)/shard_map/ppermute | solution.py:434
  49.4 11.4 %collective-permute-start.15 = (bf16[512,256]{1,0:T(8,128)(2,1)S(1)}, bf16[512,256]{1,0:T(8,128)(2,1)S(1)}, u32[]{:S(2)}, u32[]{:S(2)}) collective-permute-start(bf16[512,256]{1,0:T(8,128)(2,1)S(1)} %fusion.33.refs_0_), channel_id=1, source_target_pairs={{0,1},{1,0},{2,3},{3,2},{4,5},{5,4},{6,7},{7,6},{8,9},{9,8},{10,11... | collective-permute-start | bytes 786440 | tf_op jit(solution)/shard_map/ppermute | solution.py:434
  49.4 9.2 %collective-permute-start.16 = (bf16[512,256]{1,0:T(8,128)(2,1)S(1)}, bf16[512,256]{1,0:T(8,128)(2,1)S(1)}, u32[]{:S(2)}, u32[]{:S(2)}) collective-permute-start(bf16[512,256]{1,0:T(8,128)(2,1)S(1)} %fusion.33.refs_0_), channel_id=1, source_target_pairs={{0,2},{1,3},{4,0},{5,1},{8,4},{9,5},{12,8},{13,9},{14,12},{15,13},... | collective-permute-start | bytes 786440 | tf_op jit(solution)/shard_map/ppermute | solution.py:434
  58.5 10.4 %collective-permute-start.18 = (bf16[512,256]{1,0:T(8,128)(2,1)S(1)}, bf16[512,256]{1,0:T(8,128)(2,1)S(1)}, u32[]{:S(2)}, u32[]{:S(2)}) collective-permute-start(bf16[512,256]{1,0:T(8,128)(2,1)S(1)} %join.20.refs_1_), channel_id=1, source_target_pairs={{0,1},{1,0},{2,3},{3,2},{4,5},{5,4},{6,7},{7,6},{8,9},{9,8},{10,11... | collective-permute-start | bytes 786440 | tf_op jit(solution)/shard_map/ppermute | solution.py:434
  58.5 10.4 %collective-permute-start.19 = (bf16[512,256]{1,0:T(8,128)(2,1)S(1)}, bf16[512,256]{1,0:T(8,128)(2,1)S(1)}, u32[]{:S(2)}, u32[]{:S(2)}) collective-permute-start(bf16[512,256]{1,0:T(8,128)(2,1)S(1)} %collective-permute-done.16.refs_2_), channel_id=1, source_target_pairs={{0,1},{1,0},{2,3},{3,2},{4,5},{5,4},{6,7},{7,6},{8,9},{9,8},{10,11... | collective-permute-start | bytes 786440 | tf_op jit(solution)/shard_map/ppermute | solution.py:434
  66.6 9.7 %collective-permute-start.17 = (bf16[512,256]{1,0:T(8,128)(2,1)S(1)}, bf16[512,256]{1,0:T(8,128)(2,1)S(1)}, u32[]{:S(2)}, u32[]{:S(2)}) collective-permute-start(bf16[512,256]{1,0:T(8,128)(2,1)S(1)} %join.21.refs_2_), channel_id=1, source_target_pairs={{0,4},{1,5},{4,8},{5,9},{8,12},{9,13},{12,14},{13,15},{14,10},{15,... | collective-permute-start | bytes 786440 | tf_op jit(solution)/shard_map/ppermute | solution.py:434
  67.0 10.6 %collective-permute-start.22 = (bf16[512,256]{1,0:T(8,128)(2,1)S(1)}, bf16[512,256]{1,0:T(8,128)(2,1)S(1)}, u32[]{:S(2)}, u32[]{:S(2)}) collective-permute-start(bf16[512,256]{1,0:T(8,128)(2,1)S(1)} %join.21.refs_2_), channel_id=1, source_target_pairs={{0,1},{1,0},{2,3},{3,2},{4,5},{5,4},{6,7},{7,6},{8,9},{9,8},{10,11... | collective-permute-start | bytes 786440 | tf_op jit(solution)/shard_map/ppermute | solution.py:434
  67.3 9.6 %collective-permute-start.24 = (bf16[512,256]{1,0:T(8,128)(2,1)S(1)}, bf16[512,256]{1,0:T(8,128)(2,1)S(1)}, u32[]{:S(2)}, u32[]{:S(2)}) collective-permute-start(bf16[512,256]{1,0:T(8,128)(2,1)S(1)} %collective-permute-done.20.refs_3_), channel_id=1, source_target_pairs={{0,2},{1,3},{4,0},{5,1},{8,4},{9,5},{12,8},{13,9},{14,12},{15,13},... | collective-permute-start | bytes 786440 | tf_op jit(solution)/shard_map/ppermute | solution.py:434
  69.0 10.2 %collective-permute-start.23 = (bf16[512,256]{1,0:T(8,128)(2,1)S(1)}, bf16[512,256]{1,0:T(8,128)(2,1)S(1)}, u32[]{:S(2)}, u32[]{:S(2)}) collective-permute-start(bf16[512,256]{1,0:T(8,128)(2,1)S(1)} %collective-permute-done.20.refs_3_), channel_id=1, source_target_pairs={{0,1},{1,0},{2,3},{3,2},{4,5},{5,4},{6,7},{7,6},{8,9},{9,8},{10,11... | collective-permute-start | bytes 786440 | tf_op jit(solution)/shard_map/ppermute | solution.py:434
  77.0 9.4 %collective-permute-start.21 = (bf16[256,256]{1,0:T(8,128)(2,1)S(1)}, bf16[256,256]{1,0:T(8,128)(2,1)S(1)}, u32[]{:S(2)}, u32[]{:S(2)}) collective-permute-start(bf16[256,256]{1,0:T(8,128)(2,1)S(1)} %slice.246), channel_id=1, source_target_pairs={{0,4},{1,5},{4,8},{5,9},{8,12},{9,13},{12,14},{13,15},{14,10},{15,... | collective-permute-start | bytes 393224 | tf_op jit(solution)/shard_map/ppermute | solution.py:434
  77.6 8.9 %collective-permute-start.27 = (bf16[256,256]{1,0:T(8,128)(2,1)S(1)}, bf16[256,256]{1,0:T(8,128)(2,1)S(1)}, u32[]{:S(2)}, u32[]{:S(2)}) collective-permute-start(bf16[256,256]{1,0:T(8,128)(2,1)S(1)} %slice.247), channel_id=1, source_target_pairs={{0,2},{1,3},{4,0},{5,1},{8,4},{9,5},{12,8},{13,9},{14,12},{15,13},... | collective-permute-start | bytes 393224 | tf_op jit(solution)/shard_map/ppermute | solution.py:434
  96.6 13.5 %collective-permute-start.30 = (f32[1,256,512]{2,1,0:T(8,128)S(1)}, f32[1,256,512]{2,1,0:T(8,128)S(1)}, u32[]{:S(2)}, u32[]{:S(2)}) collective-permute-start(f32[1,256,512]{2,1,0:T(8,128)S(1)} %join.24), channel_id=1, source_target_pairs={{0,1},{1,0},{2,3},{3,2},{4,5},{5,4},{6,7},{7,6},{8,9},{9,8},{10,11... | collective-permute-start | bytes 1572872 | tf_op jit(solution)/shard_map/ppermute | solution.py:434
  97.0 13.1 %collective-permute-start.31 = (bf16[128,512]{1,0:T(8,128)(2,1)S(1)}, bf16[128,512]{1,0:T(8,128)(2,1)S(1)}, u32[]{:S(2)}, u32[]{:S(2)}) collective-permute-start(bf16[128,512]{1,0:T(8,128)(2,1)S(1)} %get-tuple-element.111), channel_id=1, source_target_pairs={{0,4},{1,5},{4,8},{5,9},{8,12},{9,13},{12,14},{13,15},{14,10},{15,... | collective-permute-start | bytes 393224 | tf_op jit(solution)/shard_map/ppermute | solution.py:434
  100.1 10.9 %collective-permute-start.38 = (f32[1,256,512]{2,1,0:T(8,128)S(1)}, f32[1,256,512]{2,1,0:T(8,128)S(1)}, u32[]{:S(2)}, u32[]{:S(2)}) collective-permute-start(f32[1,256,512]{2,1,0:T(8,128)S(1)} %get-tuple-element.90), channel_id=1, source_target_pairs={{0,1},{1,0},{2,3},{3,2},{4,5},{5,4},{6,7},{7,6},{8,9},{9,8},{10,11... | collective-permute-start | bytes 1572872 | tf_op jit(solution)/shard_map/ppermute | solution.py:434
  100.2 11.0 %collective-permute-start.39 = (bf16[128,512]{1,0:T(8,128)(2,1)S(1)}, bf16[128,512]{1,0:T(8,128)(2,1)S(1)}, u32[]{:S(2)}, u32[]{:S(2)}) collective-permute-start(bf16[128,512]{1,0:T(8,128)(2,1)S(1)} %get-tuple-element.110), channel_id=1, source_target_pairs={{0,2},{1,3},{4,0},{5,1},{8,4},{9,5},{12,8},{13,9},{14,12},{15,13},... | collective-permute-start | bytes 393224 | tf_op jit(solution)/shard_map/ppermute | solution.py:434
  110.2 10.9 %collective-permute-start.32 = (f32[2,256,512]{2,1,0:T(8,128)S(1)}, f32[2,256,512]{2,1,0:T(8,128)S(1)}, u32[]{:S(2)}, u32[]{:S(2)}) collective-permute-start(f32[2,256,512]{2,1,0:T(8,128)S(1)} %join.25), channel_id=1, source_target_pairs={{0,1},{1,0},{2,3},{3,2},{4,5},{5,4},{6,7},{7,6},{8,9},{9,8},{10,11... | collective-permute-start | bytes 3145736 | tf_op jit(solution)/shard_map/ppermute | solution.py:434
  110.5 10.6 %collective-permute-start.33 = (bf16[256,512]{1,0:T(8,128)(2,1)S(1)}, bf16[256,512]{1,0:T(8,128)(2,1)S(1)}, u32[]{:S(2)}, u32[]{:S(2)}) collective-permute-start(bf16[256,512]{1,0:T(8,128)(2,1)S(1)} %pad_maximum_fusion.3), channel_id=1, source_target_pairs={{0,4},{1,5},{4,8},{5,9},{8,12},{9,13},{12,14},{13,15},{14,10},{15,... | collective-permute-start | bytes 786440 | tf_op jit(solution)/shard_map/ppermute | solution.py:434
  111.3 9.8 %collective-permute-start.40 = (bf16[256,512]{1,0:T(8,128)(2,1)S(1)}, bf16[256,512]{1,0:T(8,128)(2,1)S(1)}, u32[]{:S(2)}, u32[]{:S(2)}) collective-permute-start(bf16[256,512]{1,0:T(8,128)(2,1)S(1)} %pad_maximum_fusion.4), channel_id=1, source_target_pairs={{0,2},{1,3},{4,0},{5,1},{8,4},{9,5},{12,8},{13,9},{14,12},{15,13},... | collective-permute-start | bytes 786440 | tf_op jit(solution)/shard_map/ppermute | solution.py:434
  121.4 9.0 %collective-permute-start.34 = (f32[2,256,512]{2,1,0:T(8,128)S(1)}, f32[2,256,512]{2,1,0:T(8,128)S(1)}, u32[]{:S(2)}, u32[]{:S(2)}) collective-permute-start(f32[2,256,512]{2,1,0:T(8,128)S(1)} %join.26), channel_id=1, source_target_pairs={{0,1},{1,0},{2,3},{3,2},{4,5},{5,4},{6,7},{7,6},{8,9},{9,8},{10,11... | collective-permute-start | bytes 3145736 | tf_op jit(solution)/shard_map/ppermute | solution.py:434
  130.8 10.2 %collective-permute-start.36 = (f32[1,256,512]{2,1,0:T(8,128)S(1)}, f32[1,256,512]{2,1,0:T(8,128)S(1)}, u32[]{:S(2)}, u32[]{:S(2)}) collective-permute-start(f32[1,256,512]{2,1,0:T(8,128)S(1)} %join.27), channel_id=1, source_target_pairs={{0,1},{1,0},{2,3},{3,2},{4,5},{5,4},{6,7},{7,6},{8,9},{9,8},{10,11... | collective-permute-start | bytes 1572872 | tf_op jit(solution)/shard_map/ppermute | solution.py:434
  (41 other events, 274.8 us)

commit v4 on v3

--- a/solution.py
+++ b/solution.py
@@ -359,16 +359,15 @@
     depth = buf.shape[1]
     copies = []
     for i in range(n):
-
-        @pl.loop(0, 2)
-        def _(r, i=i):
-            span = rows_of(r, depth // 2)
+        for r in range(2):
+            span = slice(r * depth // 2, (r + 1) * depth // 2)
             buf[i, span, :] = jnp.dot(xt_ref[span, :], pieces[i][...], preferred_element_type=F32) * scale
-
-        copies.append(
-            pltpu.make_async_copy(buf.at[i], out_ref.at[:, block(idx_ref, i, kb)], sems.at[i])
-        )
-        copies[-1].start()
+            copies.append(
+                pltpu.make_async_copy(
+                    buf.at[i, span, :], out_ref.at[span, block(idx_ref, i, kb)], sems.at[i, r]
+                )
+            )
+            copies[-1].start()
     for copy in copies:
         copy.wait()
 
@@ -384,7 +383,7 @@
         in_specs=[IN_SMEM] + [IN_VMEM] * (n + 1) + [IN_HBM] * (not first),
         out_specs=(IN_HBM, IN_VMEM),
         input_output_aliases={} if first else {n + 2: 0},
-        scratch_shapes=[pltpu.VMEM((n, depth, kb), F32), pltpu.SemaphoreType.DMA((n,))],
+        scratch_shapes=[pltpu.VMEM((n, depth, kb), F32), pltpu.SemaphoreType.DMA((n, 2))],
         compiler_params=params(16),
         cost_estimate=cost(2 * n * depth * rows * kb, n * depth * kb * 4),
         name="gradient",

time: 183 us -> 182 us (level)
  Pallas kernels: 96.6 us -> 93.2 us
  waiting for transfers between devices: 39.2 us -> 42.3 us
    pallas_call x5, Pallas kernels: 17.8 us -> 14.4 us  [gradient(): pl.pallas_call(functools.partial(gradient_body, n, scale, first), out_sha...]
    ppermute x59, waiting for transfers between devices: 39.2 us -> 42.3 us  [send(): return lax.ppermute(a, 'layer', pairs)]
  transfers between devices with their start and end apart: 59 -> 59, of which waited for: 20 -> 22; matrix products, arithmetic and copies ran while one was open for 1% -> 1% of each run, Pallas kernels for 45% -> 44%
where the time goes in v4:
time: 182 us
  Pallas kernels  93.2 us (51%)
  waiting for transfers between devices  42.3 us (23%)
  starting transfers between devices  37.5 us (21%)
  local copies, waits for them, and re-layouts  3.75 us (2%)
  other arithmetic  3.43 us (2%)
    ppermute x59, waiting for transfers between devices, send(): return lax.ppermute(a, 'layer', pairs)  42.3 us
    ppermute x59, starting transfers between devices, send(): return lax.ppermute(a, 'layer', pairs)  37.5 us
    pallas_call x4, Pallas kernels, predict(): pl.pallas_call(functools.partial(predict_body, n, held, first), out_shape...  23.2 us
    pallas_call x3, Pallas kernels, backward(): pl.pallas_call(functools.partial(backward_body, n), out_shape=(half, half...  21.8 us
    pallas_call x5, Pallas kernels, gradient(): pl.pallas_call(functools.partial(gradient_body, n, scale, first), out_sha...  14.4 us
    pallas_call x3, Pallas kernels, hold(): pl.pallas_call(functools.partial(hold_body, n, kb), out_shape=(jax.ShapeD...  12.2 us
    pallas_call x5, Pallas kernels, project(): pl.pallas_call(functools.partial(project_body, first, sizes), out_shape=t...  6.67 us
    pallas_call x1, Pallas kernels, residuals(): pl.pallas_call(residual_body, out_shape=(jax.ShapeDtypeStruct(targets.sha...  5.35 us
  transfers between devices with their start and end apart: 59, of which 22 were waited for; matrix products, arithmetic and copies ran while one was open for 1% of the time, Pallas kernels for 44%

profile of v4, /device:TPU:0, one launch (start us, length us, event | category | flops | bytes accessed | tf_op | source)
XLA Modules:
  0.0 181.9 jit_solution(8196389589078755871)
XLA Ops:
  4.3 4.2 %start.1 = (bf16[512,1024]{1,0:T(8,128)(2,1)S(1)}, bf16[16,1024,256]{2,1,0:T(8,128)(2,1)S(1)}) custom-call(s32[16]{0:T(128)S(1)} %stack.147.idx_ref, bf16[512,2048]{1,0:T(8,128)(2,1)S(1)} %fusion.hot_ref, bf16[2048,1024]{1,0:T(8,128)(2,1)S(1)} %copy-done.2, bf16[1024,4096]{1,0:T(8,128)(2,1)} %basis_ref.1), custom_call_target="tpu_custom_call" | custom-call | flops 2147483648 | bytes 4194304 | tf_op jit(solution)/shard_map/start/pallas_call | solution.py:72
  11.9 3.0 %collective-permute-start.2 = (f16[256,256]{1,0:T(8,128)(2,1)S(1)}, f16[256,256]{1,0:T(8,128)(2,1)S(1)}, u32[]{:S(2)}, u32[]{:S(2)}) collective-permute-start(f16[256,256]{1,0:T(8,128)(2,1)S(1)} %get-tuple-element.113), channel_id=1, source_target_pairs={{0,4},{1,5},{4,8},{5,9},{8,12},{9,13},{12,14},{13,15},{14,10},{15,... | collective-permute-start | bytes 393224 | tf_op jit(solution)/shard_map/ppermute | solution.py:433
  21.2 4.1 %hold.4 = (bf16[8,512,1024]{2,1,0:T(8,128)(2,1)S(1)}, f32[8,128]{1,0:T(8,128)S(1)}) custom-call(s32[2]{0:T(128)S(1)} %pad_add_fusion.1.idx_ref, bf16[8,4096,1024]{2,1,0:T(8,128)(2,1)} %coeff_ref.19, f32[8,128]{1,0:T(8,128)S(1)} %slice_convert_fusion.10.mark_ref.after_ref), custom_call_target="tpu_custom_call" | custom-call | bytes 8388608 | tf_op jit(solution)/shard_map/hold/pallas_call | solution.py:225
  31.8 4.1 %hold.3 = (bf16[8,512,1024]{2,1,0:T(8,128)(2,1)S(1)}, f32[8,128]{1,0:T(8,128)S(1)}) custom-call(s32[2]{0:T(128)S(1)} %pad_add_fusion.idx_ref, bf16[8,4096,1024]{2,1,0:T(8,128)(2,1)} %coeff_ref.19, f32[8,128]{1,0:T(8,128)S(1)} %slice_convert_fusion.9.after_ref.mark_ref), custom_call_target="tpu_custom_call" | custom-call | bytes 8388608 | tf_op jit(solution)/shard_map/hold/pallas_call | solution.py:225
  40.9 6.6 %collective-permute-done.12 = f16[512,256]{1,0:T(8,128)(2,1)S(1)} collective-permute-done((f16[512,256]{1,0:T(8,128)(2,1)S(1)}, f16[512,256]{1,0:T(8,128)(2,1)S(1)}, u32[]{:S(2)}, u32[]{:S(2)}) %collective-permute-start.12) | collective-permute-done | bytes 262176 | tf_op jit(solution)/shard_map/ppermute | solution.py:433
  51.2 2.8 %predict.4 = (f32[512,1024]{1,0:T(8,128)S(1)}, f32[8,128]{1,0:T(8,128)S(1)}) custom-call(s32[1]{0:T(128)} %bitcast.14.idx_ref, bf16[8,4096,1024]{2,1,0:T(8,128)(2,1)} %coeff_ref.19, bf16[512,256]{1,0:T(8,128)(2,1)S(1)} %fusion.33.refs_0_), custom_call_target="tpu_custom_call" | custom-call | flops 1073741824 | bytes 4194304 | tf_op jit(solution)/shard_map/predict/pallas_call | solution.py:200
  54.0 4.1 %hold.5 = (bf16[8,512,1024]{2,1,0:T(8,128)(2,1)S(1)}, f32[8,128]{1,0:T(8,128)S(1)}) custom-call(s32[2]{0:T(128)S(1)} %pad_add_fusion.2.idx_ref, bf16[8,4096,1024]{2,1,0:T(8,128)(2,1)} %coeff_ref.19, f32[8,128]{1,0:T(8,128)S(1)} %get-tuple-element.65.after_ref), custom_call_target="tpu_custom_call" | custom-call | bytes 8388608 | tf_op jit(solution)/shard_map/hold/pallas_call | solution.py:225
  60.7 5.7 %predict.5 = (f32[512,1024]{1,0:T(8,128)S(1)}, f32[8,128]{1,0:T(8,128)S(1)}) custom-call(s32[3]{0:T(128)S(1)} %pad_add_fusion.3.idx_ref, bf16[8,4096,1024]{2,1,0:T(8,128)(2,1)} %coeff_ref.19, bf16[512,256]{1,0:T(8,128)(2,1)S(1)} %collective-permute-done.15.refs_0_, bf16[512,256]{1,0:T(8,128)(2,1)S(1)} %join.20.refs_1_, ...), custom_call_target="tpu_custom_call", output_to_operand_aliasing={{0}: (5, {})} | custom-call | flops 3221225472 | bytes 12582912 | tf_op jit(solution)/shard_map/predict/pallas_call | solution.py:200
  69.0 7.4 %predict.6 = (f32[512,1024]{1,0:T(8,128)S(1)}, f32[8,128]{1,0:T(8,128)S(1)}) custom-call(s32[4]{0:T(128)S(1)} %pad_add_fusion.4.idx_ref, bf16[8,4096,1024]{2,1,0:T(8,128)(2,1)} %coeff_ref.19, bf16[512,256]{1,0:T(8,128)(2,1)S(1)} %collective-permute-done.18.refs_0_, ...), custom_call_target="tpu_custom_call", output_to_operand_aliasing={{0}: (6, {})} | custom-call | flops 4294967296 | bytes 16777216 | tf_op jit(solution)/shard_map/predict/pallas_call | solution.py:200
  79.2 7.3 %predict.7 = (f32[512,1024]{1,0:T(8,128)S(1)}, f32[8,128]{1,0:T(8,128)S(1)}) custom-call(s32[2]{0:T(128)S(1)} %pad_add_fusion.5.idx_ref, bf16[8,4096,1024]{2,1,0:T(8,128)(2,1)} %coeff_ref.19, bf16[512,256]{1,0:T(8,128)(2,1)S(1)} %collective-permute-done.22.refs_0_, ...), custom_call_target="tpu_custom_call", output_to_operand_aliasing={{0}: (10, {})} | custom-call | flops 6442450944 | bytes 8388608 | tf_op jit(solution)/shard_map/predict/pallas_call | solution.py:200
  88.1 5.4 %residuals.1 = (f32[8,64,1024]{2,1,0:T(8,128)}, bf16[512,1024]{1,0:T(8,128)(2,1)S(1)}, f32[1,256,512]{2,1,0:T(8,128)S(1)}, f32[1,256,512]{2,1,0:T(8,128)S(1)}) custom-call(bf16[512,256]{1,0:T(8,128)(2,1)S(1)} %pad_maximum_fusion.2.a_ref, bf16[512,256]{1,0:T(8,128)(2,1)S(1)} %collective-permute-done.28.b_ref, ...), custom_call_target="tpu_custom_call" | custom-call | flops 4294967296 | bytes 8388608 | tf_op jit(solution)/shard_map/residuals/pallas_call | solution.py:278
  93.8 2.6 %backward_held.3 = (f32[1,256,512]{2,1,0:T(8,128)S(1)}, f32[1,256,512]{2,1,0:T(8,128)S(1)}) custom-call(bf16[512,1024]{1,0:T(8,128)(2,1)S(1)} %get-tuple-element.78.low_ref, f32[1,256,512]{2,1,0:T(8,128)S(1)} %get-tuple-element.79.mark_ref, bf16[8,512,1024]{2,1,0:T(8,128)(2,1)S(1)} %get-tuple-element.71.refs_6_.refs_0_), custom_call_target="tpu_custom_call" | custom-call | flops 2147483648 | bytes 8388608 | tf_op jit(solution)/shard_map/backward_held/pallas_call | solution.py:344
  97.5 2.6 %backward_held.2 = (f32[1,256,512]{2,1,0:T(8,128)S(1)}, f32[1,256,512]{2,1,0:T(8,128)S(1)}) custom-call(bf16[512,1024]{1,0:T(8,128)(2,1)S(1)} %get-tuple-element.78.low_ref, f32[8,128]{1,0:T(8,128)S(1)} %slice_convert_fusion.7.mark_ref, bf16[8,512,1024]{2,1,0:T(8,128)(2,1)S(1)} %get-tuple-element.72.refs_7_.refs_0_), custom_call_target="tpu_custom_call" | custom-call | flops 2147483648 | bytes 8388608 | tf_op jit(solution)/shard_map/backward_held/pallas_call | solution.py:344
  101.8 8.2 %backward.3 = (f32[2,256,512]{2,1,0:T(8,128)S(1)}, f32[2,256,512]{2,1,0:T(8,128)S(1)}) custom-call(s32[4]{0:T(128)S(1)} %pad_add_fusion.7.idx_ref, bf16[8,4096,1024]{2,1,0:T(8,128)(2,1)} %coeff_ref.19, bf16[512,1024]{1,0:T(8,128)(2,1)S(1)} %get-tuple-element.78.low_ref, f32[1,256,512]{2,1,0:T(8,128)S(1)} %get-tuple-element.81.mark_ref), custom_call_target="tpu_custom_call" | custom-call | flops 4294967296 | bytes 16777216 | tf_op jit(solution)/shard_map/backward/pallas_call | solution.py:314
  112.8 8.2 %backward.5 = (f32[2,256,512]{2,1,0:T(8,128)S(1)}, f32[2,256,512]{2,1,0:T(8,128)S(1)}) custom-call(s32[4]{0:T(128)S(1)} %pad_add_fusion.8.idx_ref, bf16[8,4096,1024]{2,1,0:T(8,128)(2,1)} %coeff_ref.19, bf16[512,1024]{1,0:T(8,128)(2,1)S(1)} %get-tuple-element.78.low_ref, f32[8,128]{1,0:T(8,128)S(1)} %slice_convert_fusion.6.mark_ref), custom_call_target="tpu_custom_call" | custom-call | flops 4294967296 | bytes 16777216 | tf_op jit(solution)/shard_map/backward/pallas_call | solution.py:314
  123.7 5.3 %backward.4 = (f32[1,256,512]{2,1,0:T(8,128)S(1)}, f32[1,256,512]{2,1,0:T(8,128)S(1)}) custom-call(s32[2]{0:T(128)S(1)} %pad_add_fusion.6.idx_ref, bf16[8,4096,1024]{2,1,0:T(8,128)(2,1)} %coeff_ref.19, bf16[512,1024]{1,0:T(8,128)(2,1)S(1)} %get-tuple-element.78.low_ref, f32[8,128]{1,0:T(8,128)S(1)} %slice_convert_fusion.5.mark_ref), custom_call_target="tpu_custom_call" | custom-call | flops 2147483648 | bytes 8388608 | tf_op jit(solution)/shard_map/backward/pallas_call | solution.py:314
  132.9 6.6 %collective-permute-done.37.right_ref = bf16[256,512]{1,0:T(8,128)(2,1)S(1)} collective-permute-done((bf16[256,512]{1,0:T(8,128)(2,1)S(1)}, bf16[256,512]{1,0:T(8,128)(2,1)S(1)}, u32[]{:S(2)}, u32[]{:S(2)}) %collective-permute-start.37) | collective-permute-done | bytes 262176 | tf_op jit(solution)/shard_map/ppermute | solution.py:433
  146.2 3.7 %collective-permute-done.43.value_ref = bf16[512,256]{1,0:T(8,128)(2,1)S(1)} collective-permute-done((bf16[512,256]{1,0:T(8,128)(2,1)S(1)}, bf16[512,256]{1,0:T(8,128)(2,1)S(1)}, u32[]{:S(2)}, u32[]{:S(2)}) %collective-permute-start.43) | collective-permute-done | bytes 262176 | tf_op jit(solution)/shard_map/ppermute | solution.py:433
  153.3 3.1 %gradient.6 = (f32[1024,4096]{1,0:T(8,128)}, f32[8,128]{1,0:T(8,128)S(1)}) custom-call(s32[4]{0:T(128)S(1)} %pad_add_fusion.9.idx_ref, bf16[1024,512]{1,0:T(8,128)(2,1)S(1)} %bitcast.116, bf16[512,256]{1,0:T(8,128)(2,1)S(1)} %join.28.refs_0_, bf16[512,256]{1,0:T(8,128)(2,1)S(1)} %collective-permute-done.46.refs_1_, ...), custom_call_target="tpu_custom_call", output_to_operand_aliasing={{0}: (6, {})} | custom-call | flops 1073741824 | bytes 4194304 | tf_op jit(solution)/shard_map/gradient/pallas_call | solution.py:380
  156.3 3.5 %collective-permute-done.45.value_ref = bf16[512,256]{1,0:T(8,128)(2,1)S(1)} collective-permute-done((bf16[512,256]{1,0:T(8,128)(2,1)S(1)}, bf16[512,256]{1,0:T(8,128)(2,1)S(1)}, u32[]{:S(2)}, u32[]{:S(2)}) %collective-permute-start.45) | collective-permute-done | bytes 262176 | tf_op jit(solution)/shard_map/ppermute | solution.py:433
  163.3 3.1 %gradient.7 = (f32[1024,4096]{1,0:T(8,128)}, f32[8,128]{1,0:T(8,128)S(1)}) custom-call(s32[4]{0:T(128)S(1)} %pad_add_fusion.10.idx_ref, bf16[1024,512]{1,0:T(8,128)(2,1)S(1)} %bitcast.117, bf16[512,256]{1,0:T(8,128)(2,1)S(1)} %join.29.refs_0_, bf16[512,256]{1,0:T(8,128)(2,1)S(1)} %collective-permute-done.50.refs_1_, ...), custom_call_target="tpu_custom_call", output_to_operand_aliasing={{0}: (6, {})} | custom-call | flops 1073741824 | bytes 4194304 | tf_op jit(solution)/shard_map/gradient/pallas_call | solution.py:380
  166.3 3.5 %collective-permute-done.49.value_ref = bf16[512,256]{1,0:T(8,128)(2,1)S(1)} collective-permute-done((bf16[512,256]{1,0:T(8,128)(2,1)S(1)}, bf16[512,256]{1,0:T(8,128)(2,1)S(1)}, u32[]{:S(2)}, u32[]{:S(2)}) %collective-permute-start.49) | collective-permute-done | bytes 262176 | tf_op jit(solution)/shard_map/ppermute | solution.py:433
  173.2 3.1 %gradient.8 = (f32[1024,4096]{1,0:T(8,128)}, f32[8,128]{1,0:T(8,128)S(1)}) custom-call(s32[4]{0:T(128)S(1)} %pad_add_fusion.11.idx_ref, bf16[1024,512]{1,0:T(8,128)(2,1)S(1)} %bitcast.118, bf16[512,256]{1,0:T(8,128)(2,1)S(1)} %join.30.refs_0_, bf16[512,256]{1,0:T(8,128)(2,1)S(1)} %collective-permute-done.54.refs_1_, ...), custom_call_target="tpu_custom_call", output_to_operand_aliasing={{0}: (6, {})} | custom-call | flops 1073741824 | bytes 4194304 | tf_op jit(solution)/shard_map/gradient/pallas_call | solution.py:380
  178.9 2.9 %gradient.9 = (f32[1024,4096]{1,0:T(8,128)}, f32[8,128]{1,0:T(8,128)}) custom-call(s32[2]{0:T(128)S(1)} %copy-done.4, bf16[1024,512]{1,0:T(8,128)(2,1)S(1)} %bitcast.119, bf16[512,256]{1,0:T(8,128)(2,1)S(1)} %pad_maximum_fusion.5.refs_0_, bf16[512,256]{1,0:T(8,128)(2,1)S(1)} %collective-permute-done.58.refs_1_, ...), custom_call_target="tpu_custom_call", output_to_operand_aliasing={{0}: (4, {})} | custom-call | flops 536870912 | bytes 2097152 | tf_op jit(solution)/shard_map/gradient/pallas_call | solution.py:380
  (201 shorter events, 69.1 us)
Async XLA Ops:
  18.7 10.7 %collective-permute-start.3 = (f32[2,512,256]{2,1,0:T(8,128)S(1)}, f32[2,512,256]{2,1,0:T(8,128)S(1)}, u32[]{:S(2)}, u32[]{:S(2)}) collective-permute-start(f32[2,512,256]{2,1,0:T(8,128)S(1)} %join.17), channel_id=1, source_target_pairs={{0,1},{1,0},{2,3},{3,2},{4,5},{5,4},{6,7},{7,6},{8,9},{9,8},{10,11... | collective-permute-start | bytes 3145736 | tf_op jit(solution)/shard_map/ppermute | solution.py:433
  18.8 8.8 %collective-permute-start.4 = (f16[512,256]{1,0:T(8,128)(2,1)S(1)}, f16[512,256]{1,0:T(8,128)(2,1)S(1)}, u32[]{:S(2)}, u32[]{:S(2)}) collective-permute-start(f16[512,256]{1,0:T(8,128)(2,1)S(1)} %pad_maximum_fusion), channel_id=1, source_target_pairs={{0,4},{1,5},{4,8},{5,9},{8,12},{9,13},{12,14},{13,15},{14,10},{15,... | collective-permute-start | bytes 786440 | tf_op jit(solution)/shard_map/ppermute | solution.py:433
  29.6 8.8 %collective-permute-start.5 = (f32[2,512,256]{2,1,0:T(8,128)S(1)}, f32[2,512,256]{2,1,0:T(8,128)S(1)}, u32[]{:S(2)}, u32[]{:S(2)}) collective-permute-start(f32[2,512,256]{2,1,0:T(8,128)S(1)} %join.18), channel_id=1, source_target_pairs={{0,1},{1,0},{2,3},{3,2},{4,5},{5,4},{6,7},{7,6},{8,9},{9,8},{10,11... | collective-permute-start | bytes 3145736 | tf_op jit(solution)/shard_map/ppermute | solution.py:433
  38.7 10.2 %collective-permute-start.7 = (f32[1,512,256]{2,1,0:T(8,128)S(1)}, f32[1,512,256]{2,1,0:T(8,128)S(1)}, u32[]{:S(2)}, u32[]{:S(2)}) collective-permute-start(f32[1,512,256]{2,1,0:T(8,128)S(1)} %join.19), channel_id=1, source_target_pairs={{0,1},{1,0},{2,3},{3,2},{4,5},{5,4},{6,7},{7,6},{8,9},{9,8},{10,11... | collective-permute-start | bytes 1572872 | tf_op jit(solution)/shard_map/ppermute | solution.py:433
  49.0 9.1 %collective-permute-start.13 = (bf16[512,256]{1,0:T(8,128)(2,1)S(1)}, bf16[512,256]{1,0:T(8,128)(2,1)S(1)}, u32[]{:S(2)}, u32[]{:S(2)}) collective-permute-start(bf16[512,256]{1,0:T(8,128)(2,1)S(1)} %fusion.33.refs_0_), channel_id=1, source_target_pairs={{0,4},{1,5},{4,8},{5,9},{8,12},{9,13},{12,14},{13,15},{14,10},{15,... | collective-permute-start | bytes 786440 | tf_op jit(solution)/shard_map/ppermute | solution.py:433
  49.4 11.4 %collective-permute-start.15 = (bf16[512,256]{1,0:T(8,128)(2,1)S(1)}, bf16[512,256]{1,0:T(8,128)(2,1)S(1)}, u32[]{:S(2)}, u32[]{:S(2)}) collective-permute-start(bf16[512,256]{1,0:T(8,128)(2,1)S(1)} %fusion.33.refs_0_), channel_id=1, source_target_pairs={{0,1},{1,0},{2,3},{3,2},{4,5},{5,4},{6,7},{7,6},{8,9},{9,8},{10,11... | collective-permute-start | bytes 786440 | tf_op jit(solution)/shard_map/ppermute | solution.py:433
  49.4 9.2 %collective-permute-start.16 = (bf16[512,256]{1,0:T(8,128)(2,1)S(1)}, bf16[512,256]{1,0:T(8,128)(2,1)S(1)}, u32[]{:S(2)}, u32[]{:S(2)}) collective-permute-start(bf16[512,256]{1,0:T(8,128)(2,1)S(1)} %fusion.33.refs_0_), channel_id=1, source_target_pairs={{0,2},{1,3},{4,0},{5,1},{8,4},{9,5},{12,8},{13,9},{14,12},{15,13},... | collective-permute-start | bytes 786440 | tf_op jit(solution)/shard_map/ppermute | solution.py:433
  58.5 10.4 %collective-permute-start.18 = (bf16[512,256]{1,0:T(8,128)(2,1)S(1)}, bf16[512,256]{1,0:T(8,128)(2,1)S(1)}, u32[]{:S(2)}, u32[]{:S(2)}) collective-permute-start(bf16[512,256]{1,0:T(8,128)(2,1)S(1)} %join.20.refs_1_), channel_id=1, source_target_pairs={{0,1},{1,0},{2,3},{3,2},{4,5},{5,4},{6,7},{7,6},{8,9},{9,8},{10,11... | collective-permute-start | bytes 786440 | tf_op jit(solution)/shard_map/ppermute | solution.py:433
  58.5 10.4 %collective-permute-start.19 = (bf16[512,256]{1,0:T(8,128)(2,1)S(1)}, bf16[512,256]{1,0:T(8,128)(2,1)S(1)}, u32[]{:S(2)}, u32[]{:S(2)}) collective-permute-start(bf16[512,256]{1,0:T(8,128)(2,1)S(1)} %collective-permute-done.16.refs_2_), channel_id=1, source_target_pairs={{0,1},{1,0},{2,3},{3,2},{4,5},{5,4},{6,7},{7,6},{8,9},{9,8},{10,11... | collective-permute-start | bytes 786440 | tf_op jit(solution)/shard_map/ppermute | solution.py:433
  66.6 9.7 %collective-permute-start.17 = (bf16[512,256]{1,0:T(8,128)(2,1)S(1)}, bf16[512,256]{1,0:T(8,128)(2,1)S(1)}, u32[]{:S(2)}, u32[]{:S(2)}) collective-permute-start(bf16[512,256]{1,0:T(8,128)(2,1)S(1)} %join.21.refs_2_), channel_id=1, source_target_pairs={{0,4},{1,5},{4,8},{5,9},{8,12},{9,13},{12,14},{13,15},{14,10},{15,... | collective-permute-start | bytes 786440 | tf_op jit(solution)/shard_map/ppermute | solution.py:433
  67.0 10.6 %collective-permute-start.22 = (bf16[512,256]{1,0:T(8,128)(2,1)S(1)}, bf16[512,256]{1,0:T(8,128)(2,1)S(1)}, u32[]{:S(2)}, u32[]{:S(2)}) collective-permute-start(bf16[512,256]{1,0:T(8,128)(2,1)S(1)} %join.21.refs_2_), channel_id=1, source_target_pairs={{0,1},{1,0},{2,3},{3,2},{4,5},{5,4},{6,7},{7,6},{8,9},{9,8},{10,11... | collective-permute-start | bytes 786440 | tf_op jit(solution)/shard_map/ppermute | solution.py:433
  67.3 9.6 %collective-permute-start.24 = (bf16[512,256]{1,0:T(8,128)(2,1)S(1)}, bf16[512,256]{1,0:T(8,128)(2,1)S(1)}, u32[]{:S(2)}, u32[]{:S(2)}) collective-permute-start(bf16[512,256]{1,0:T(8,128)(2,1)S(1)} %collective-permute-done.20.refs_3_), channel_id=1, source_target_pairs={{0,2},{1,3},{4,0},{5,1},{8,4},{9,5},{12,8},{13,9},{14,12},{15,13},... | collective-permute-start | bytes 786440 | tf_op jit(solution)/shard_map/ppermute | solution.py:433
  69.0 10.2 %collective-permute-start.23 = (bf16[512,256]{1,0:T(8,128)(2,1)S(1)}, bf16[512,256]{1,0:T(8,128)(2,1)S(1)}, u32[]{:S(2)}, u32[]{:S(2)}) collective-permute-start(bf16[512,256]{1,0:T(8,128)(2,1)S(1)} %collective-permute-done.20.refs_3_), channel_id=1, source_target_pairs={{0,1},{1,0},{2,3},{3,2},{4,5},{5,4},{6,7},{7,6},{8,9},{9,8},{10,11... | collective-permute-start | bytes 786440 | tf_op jit(solution)/shard_map/ppermute | solution.py:433
  77.0 9.4 %collective-permute-start.21 = (bf16[256,256]{1,0:T(8,128)(2,1)S(1)}, bf16[256,256]{1,0:T(8,128)(2,1)S(1)}, u32[]{:S(2)}, u32[]{:S(2)}) collective-permute-start(bf16[256,256]{1,0:T(8,128)(2,1)S(1)} %slice.246), channel_id=1, source_target_pairs={{0,4},{1,5},{4,8},{5,9},{8,12},{9,13},{12,14},{13,15},{14,10},{15,... | collective-permute-start | bytes 393224 | tf_op jit(solution)/shard_map/ppermute | solution.py:433
  77.6 8.9 %collective-permute-start.27 = (bf16[256,256]{1,0:T(8,128)(2,1)S(1)}, bf16[256,256]{1,0:T(8,128)(2,1)S(1)}, u32[]{:S(2)}, u32[]{:S(2)}) collective-permute-start(bf16[256,256]{1,0:T(8,128)(2,1)S(1)} %slice.247), channel_id=1, source_target_pairs={{0,2},{1,3},{4,0},{5,1},{8,4},{9,5},{12,8},{13,9},{14,12},{15,13},... | collective-permute-start | bytes 393224 | tf_op jit(solution)/shard_map/ppermute | solution.py:433
  96.6 13.5 %collective-permute-start.30 = (f32[1,256,512]{2,1,0:T(8,128)S(1)}, f32[1,256,512]{2,1,0:T(8,128)S(1)}, u32[]{:S(2)}, u32[]{:S(2)}) collective-permute-start(f32[1,256,512]{2,1,0:T(8,128)S(1)} %join.24), channel_id=1, source_target_pairs={{0,1},{1,0},{2,3},{3,2},{4,5},{5,4},{6,7},{7,6},{8,9},{9,8},{10,11... | collective-permute-start | bytes 1572872 | tf_op jit(solution)/shard_map/ppermute | solution.py:433
  97.0 13.1 %collective-permute-start.31 = (bf16[128,512]{1,0:T(8,128)(2,1)S(1)}, bf16[128,512]{1,0:T(8,128)(2,1)S(1)}, u32[]{:S(2)}, u32[]{:S(2)}) collective-permute-start(bf16[128,512]{1,0:T(8,128)(2,1)S(1)} %get-tuple-element.111), channel_id=1, source_target_pairs={{0,4},{1,5},{4,8},{5,9},{8,12},{9,13},{12,14},{13,15},{14,10},{15,... | collective-permute-start | bytes 393224 | tf_op jit(solution)/shard_map/ppermute | solution.py:433
  100.1 10.9 %collective-permute-start.38 = (f32[1,256,512]{2,1,0:T(8,128)S(1)}, f32[1,256,512]{2,1,0:T(8,128)S(1)}, u32[]{:S(2)}, u32[]{:S(2)}) collective-permute-start(f32[1,256,512]{2,1,0:T(8,128)S(1)} %get-tuple-element.90), channel_id=1, source_target_pairs={{0,1},{1,0},{2,3},{3,2},{4,5},{5,4},{6,7},{7,6},{8,9},{9,8},{10,11... | collective-permute-start | bytes 1572872 | tf_op jit(solution)/shard_map/ppermute | solution.py:433
  100.2 11.0 %collective-permute-start.39 = (bf16[128,512]{1,0:T(8,128)(2,1)S(1)}, bf16[128,512]{1,0:T(8,128)(2,1)S(1)}, u32[]{:S(2)}, u32[]{:S(2)}) collective-permute-start(bf16[128,512]{1,0:T(8,128)(2,1)S(1)} %get-tuple-element.110), channel_id=1, source_target_pairs={{0,2},{1,3},{4,0},{5,1},{8,4},{9,5},{12,8},{13,9},{14,12},{15,13},... | collective-permute-start | bytes 393224 | tf_op jit(solution)/shard_map/ppermute | solution.py:433
  110.2 10.9 %collective-permute-start.32 = (f32[2,256,512]{2,1,0:T(8,128)S(1)}, f32[2,256,512]{2,1,0:T(8,128)S(1)}, u32[]{:S(2)}, u32[]{:S(2)}) collective-permute-start(f32[2,256,512]{2,1,0:T(8,128)S(1)} %join.25), channel_id=1, source_target_pairs={{0,1},{1,0},{2,3},{3,2},{4,5},{5,4},{6,7},{7,6},{8,9},{9,8},{10,11... | collective-permute-start | bytes 3145736 | tf_op jit(solution)/shard_map/ppermute | solution.py:433
  110.5 10.6 %collective-permute-start.33 = (bf16[256,512]{1,0:T(8,128)(2,1)S(1)}, bf16[256,512]{1,0:T(8,128)(2,1)S(1)}, u32[]{:S(2)}, u32[]{:S(2)}) collective-permute-start(bf16[256,512]{1,0:T(8,128)(2,1)S(1)} %pad_maximum_fusion.3), channel_id=1, source_target_pairs={{0,4},{1,5},{4,8},{5,9},{8,12},{9,13},{12,14},{13,15},{14,10},{15,... | collective-permute-start | bytes 786440 | tf_op jit(solution)/shard_map/ppermute | solution.py:433
  111.3 9.8 %collective-permute-start.40 = (bf16[256,512]{1,0:T(8,128)(2,1)S(1)}, bf16[256,512]{1,0:T(8,128)(2,1)S(1)}, u32[]{:S(2)}, u32[]{:S(2)}) collective-permute-start(bf16[256,512]{1,0:T(8,128)(2,1)S(1)} %pad_maximum_fusion.4), channel_id=1, source_target_pairs={{0,2},{1,3},{4,0},{5,1},{8,4},{9,5},{12,8},{13,9},{14,12},{15,13},... | collective-permute-start | bytes 786440 | tf_op jit(solution)/shard_map/ppermute | solution.py:433
  121.4 9.0 %collective-permute-start.34 = (f32[2,256,512]{2,1,0:T(8,128)S(1)}, f32[2,256,512]{2,1,0:T(8,128)S(1)}, u32[]{:S(2)}, u32[]{:S(2)}) collective-permute-start(f32[2,256,512]{2,1,0:T(8,128)S(1)} %join.26), channel_id=1, source_target_pairs={{0,1},{1,0},{2,3},{3,2},{4,5},{5,4},{6,7},{7,6},{8,9},{9,8},{10,11... | collective-permute-start | bytes 3145736 | tf_op jit(solution)/shard_map/ppermute | solution.py:433
  130.8 10.2 %collective-permute-start.36 = (f32[1,256,512]{2,1,0:T(8,128)S(1)}, f32[1,256,512]{2,1,0:T(8,128)S(1)}, u32[]{:S(2)}, u32[]{:S(2)}) collective-permute-start(f32[1,256,512]{2,1,0:T(8,128)S(1)} %join.27), channel_id=1, source_target_pairs={{0,1},{1,0},{2,3},{3,2},{4,5},{5,4},{6,7},{7,6},{8,9},{9,8},{10,11... | collective-permute-start | bytes 1572872 | tf_op jit(solution)/shard_map/ppermute | solution.py:433
  (41 other events, 274.6 us)
